TPU v7x, 256 devices: a whole 4x4x8 slice. The times are simulated.
256 devices in a mesh: replica: 2 (over x_lo), head: 8 (over z), blk: 16 (over y, x_hi, core).
Axes of the slice: x: 4 (x_hi: 2, x_lo: 2; x = x_hi * 2 + x_lo), y: 4, z: 8, core: 2. Of those that a mesh axis runs over, the one named last changes fastest.
Arguments:
- nodes: float32 [65536, 512], P(('replica', 'blk'))
- w_query: float32 [512, 512], P(None, 'head'), may hold values from -0.25 to 0.25
- w_key: float32 [512, 512], P(None, 'head'), may hold values from -0.25 to 0.25
- w_value: float32 [512, 512], P(None, 'head'), may hold values from -0.25 to 0.25
- w_out: float32 [512, 512], P('head'), may hold values from -0.25 to 0.25
- tile_cols: int32 [256, 4], P(('replica', 'blk')), may hold values from 0 to 255, as said below
- tile_masks: int32 [256, 4, 256, 256], P(('replica', 'blk')), may hold values 0 or 1
Outputs:
- updated: float32 [65536, 512], P(('replica', 'blk'), 'head')
- log_sums: float32 [65536, 8], P(('replica', 'blk'), 'head')
Inputs may be any that keep to these rules, and one draw needn't show every extreme that they name: `tile_cols`: entry 0 of row a is a; the 4 entries of a row are distinct.
All inputs are finite; a program needn't handle non-finite values. No bound on the sum of `tile_masks` on one device may be relied on, other than what follows from the above.
Results may differ from a plain program's by a relative error of at most 0.0003.
Values sent between devices are 32-bit elements; how exact they have to be, the bound alone decides.
A program may use at most 192 MiB of HBM per device.

v0:
```python
import jax
import jax.numpy as jnp
from jax import lax
from jax.sharding import PartitionSpec as P

HD = 64


def passed_along(block, axis, distance):
    devices = range(lax.axis_size(axis))
    route = [((i - distance) % len(devices), i) for i in devices]
    return lax.ppermute(block, axis, route)


def edge_table(tile_masks):
    count_rows = tile_masks.shape[2]
    eye_table = jnp.eye(count_rows, dtype=jnp.float32)
    first_tile = (jnp.arange(tile_masks.shape[1]) == 0).astype(jnp.float32)
    return jnp.maximum(
        tile_masks.astype(jnp.float32), first_tile[None, :, None, None] * eye_table[None, None]
    )


def body(nodes, w_query, w_key, w_value, w_out, tile_cols, tile_masks):
    highest = lax.Precision.HIGHEST
    row_count = nodes.shape[0]
    block_rows = tile_masks.shape[2]
    block_count = row_count // block_rows
    tile_count = tile_masks.shape[1]
    head_width = HD
    local_heads = w_query.shape[1] // head_width
    split_at = local_heads * head_width
    score_scale = 1.0 / head_width**0.5
    queries = jnp.dot(
        nodes, w_query, precision=highest, preferred_element_type=jnp.float32
    ).reshape(block_count, block_rows, local_heads, head_width)
    key_part = jnp.dot(nodes, w_key, precision=highest, preferred_element_type=jnp.float32)
    value_part = jnp.dot(nodes, w_value, precision=highest, preferred_element_type=jnp.float32)
    panel_own = jnp.concatenate([key_part, value_part], axis=1)
    edges = edge_table(tile_masks)
    replicas = lax.axis_size("replica")
    cycle_size = lax.axis_size("blk")
    blk_here = lax.axis_index("blk")

    def collect(tiles, piece, first_block):
        piece_blocks = piece.shape[0] // block_rows
        blocks = piece.reshape(piece_blocks, block_rows, piece.shape[1])
        local = tile_cols - first_block
        inside = (local >= 0) & (local < piece_blocks)
        picked = blocks[jnp.clip(local, 0, piece_blocks - 1)]
        return jnp.where(inside[:, :, None, None], picked, tiles)

    def visit_panel(tiles, panel, group):
        for replica_index in range(replicas):
            piece = panel[replica_index * row_count : (replica_index + 1) * row_count]
            tiles = collect(tiles, piece, (replica_index * cycle_size + group) * block_count)
        return tiles

    start_tiles = jnp.zeros((block_count, tile_count, block_rows, 2 * split_at), jnp.float32)
    panel_start = lax.all_gather(panel_own, "replica", axis=0, tiled=True)
    first_tiles = visit_panel(start_tiles, panel_start, blk_here)

    def turn(turn_index, carry):
        tiles, panel = carry
        panel = passed_along(panel, "blk", 1)
        group = (blk_here - turn_index - 1) % cycle_size
        return (visit_panel(tiles, panel, group), panel)

    final_tiles, unused_panel = lax.fori_loop(0, cycle_size - 1, turn, (first_tiles, panel_start))
    keys_now = final_tiles[..., :split_at].reshape(
        block_count, tile_count, block_rows, local_heads, head_width
    )
    values_now = final_tiles[..., split_at:].reshape(
        block_count, tile_count, block_rows, local_heads, head_width
    )
    live = edges[None] > 0.5
    scores = jnp.einsum("aihd,atjhd->hatij", queries, keys_now, precision=highest) * score_scale
    scores = jnp.where(live, scores, -1e30)
    top_score = jnp.max(scores, axis=(2, 4))
    weights = jnp.where(live, jnp.exp(scores - top_score[:, :, None, :, None]), 0.0)
    totals = jnp.sum(weights, axis=(2, 4))
    attended = (
        jnp.einsum("hatij,atjhd->haid", weights, values_now, precision=highest)
        / totals[:, :, :, None]
    )
    log_sum = (top_score + jnp.log(totals)).reshape(local_heads, row_count)
    merged = attended.transpose(1, 2, 0, 3).reshape(row_count, split_at)
    term = jnp.dot(merged, w_out, precision=highest, preferred_element_type=jnp.float32)
    mixed = lax.psum_scatter(term, "head", scatter_dimension=1, tiled=True)
    width_here = mixed.shape[1]
    residual = lax.dynamic_slice_in_dim(nodes, lax.axis_index("head") * width_here, width_here, 1)
    return (residual + mixed, log_sum.T)


def solution(mesh):
    placed = (
        P(("replica", "blk"), None),
        P(None, "head"),
        P(None, "head"),
        P(None, "head"),
        P("head", None),
        P(("replica", "blk"), None),
        P(("replica", "blk"), None, None, None),
    )
    return jax.shard_map(
        body,
        mesh=mesh,
        in_specs=placed,
        out_specs=(P(("replica", "blk"), "head"), P(("replica", "blk"), "head")),
        check_vma=False,
    )
```

profile of v0, /device:TPU:1, one launch (start us, length us, event | category | flops | bytes accessed | tf_op | source)
XLA Modules:
  0.0 895.6 jit_solution(7636561567958968333)
XLA Ops:
  27.5 9.2 %copy.31 = s32[8,4,256,256]{2,3,1,0:T(8,128)} copy(s32[8,4,256,256]{3,2,1,0:T(8,128)} %param.15) | data formatting | bytes 16777216 | tf_op args[6]
  37.0 24.3 %all-gather.2.cloned.1.call-done = f32[4096,128]{0,1:T(8,128)} async-done(((f32[2048,128]{0,1:T(8,128)}), f32[4096,128]{0,1:T(8,128)}) %all-gather.2.cloned.1.call-update) | async-done | bytes 2097168 | tf_op jit(solution)/shard_map/all_gather | solution.py:60
  80.1 695.3 %while.17 = (s32[]{:T(128)}, f32[8,4,256,128]{3,2,1,0:T(8,128)}, f32[4096,128]{1,0:T(8,128)}, s32[]{:T(128)}, s32[8,4]{0,1:T(4,128)S(1)}, /*index=5*/s32[]{:T(12...) while((s32[]{:T(128)}, f32[8,4,256,128]{3,2,1,0:T(8,128)}, f32[4096,128]{1,0:T(8,128)}, ...), condition=%wide.region_1.2_spmd, body=%wide.region_0.1_spmd.sunk | while | flops 2099794 | bytes 50342476 | solution.py:69
  83.6 22.7 %collective-permute-done = f32[4096,128]{1,0:T(8,128)} collective-permute-done((f32[4096,128]{1,0:T(8,128)}, f32[4096,128]{1,0:T(8,128)}, u32[]{:S(2)}, u32[]{:S(2)}) %collective-permute-start) | collective-permute-done | bytes 2097184 | tf_op jit(solution)/shard_map/while/body/eval_jaxpr/ppermute | solution.py:12
  129.5 22.7 %collective-permute-done = f32[4096,128]{1,0:T(8,128)} collective-permute-done((f32[4096,128]{1,0:T(8,128)}, f32[4096,128]{1,0:T(8,128)}, u32[]{:S(2)}, u32[]{:S(2)}) %collective-permute-start) | collective-permute-done | bytes 2097184 | tf_op jit(solution)/shard_map/while/body/eval_jaxpr/ppermute | solution.py:12
  159.4 8.4 select_select_fusion.3
  175.4 22.7 %collective-permute-done = f32[4096,128]{1,0:T(8,128)} collective-permute-done((f32[4096,128]{1,0:T(8,128)}, f32[4096,128]{1,0:T(8,128)}, u32[]{:S(2)}, u32[]{:S(2)}) %collective-permute-start) | collective-permute-done | bytes 2097184 | tf_op jit(solution)/shard_map/while/body/eval_jaxpr/ppermute | solution.py:12
  205.3 8.4 select_select_fusion.3
  221.3 22.7 %collective-permute-done = f32[4096,128]{1,0:T(8,128)} collective-permute-done((f32[4096,128]{1,0:T(8,128)}, f32[4096,128]{1,0:T(8,128)}, u32[]{:S(2)}, u32[]{:S(2)}) %collective-permute-start) | collective-permute-done | bytes 2097184 | tf_op jit(solution)/shard_map/while/body/eval_jaxpr/ppermute | solution.py:12
  267.2 22.7 %collective-permute-done = f32[4096,128]{1,0:T(8,128)} collective-permute-done((f32[4096,128]{1,0:T(8,128)}, f32[4096,128]{1,0:T(8,128)}, u32[]{:S(2)}, u32[]{:S(2)}) %collective-permute-start) | collective-permute-done | bytes 2097184 | tf_op jit(solution)/shard_map/while/body/eval_jaxpr/ppermute | solution.py:12
  297.1 8.4 select_select_fusion.3
  313.1 22.7 %collective-permute-done = f32[4096,128]{1,0:T(8,128)} collective-permute-done((f32[4096,128]{1,0:T(8,128)}, f32[4096,128]{1,0:T(8,128)}, u32[]{:S(2)}, u32[]{:S(2)}) %collective-permute-start) | collective-permute-done | bytes 2097184 | tf_op jit(solution)/shard_map/while/body/eval_jaxpr/ppermute | solution.py:12
  343.0 8.4 select_select_fusion.3
  359.0 22.7 %collective-permute-done = f32[4096,128]{1,0:T(8,128)} collective-permute-done((f32[4096,128]{1,0:T(8,128)}, f32[4096,128]{1,0:T(8,128)}, u32[]{:S(2)}, u32[]{:S(2)}) %collective-permute-start) | collective-permute-done | bytes 2097184 | tf_op jit(solution)/shard_map/while/body/eval_jaxpr/ppermute | solution.py:12
  404.9 22.7 %collective-permute-done = f32[4096,128]{1,0:T(8,128)} collective-permute-done((f32[4096,128]{1,0:T(8,128)}, f32[4096,128]{1,0:T(8,128)}, u32[]{:S(2)}, u32[]{:S(2)}) %collective-permute-start) | collective-permute-done | bytes 2097184 | tf_op jit(solution)/shard_map/while/body/eval_jaxpr/ppermute | solution.py:12
  450.8 22.7 %collective-permute-done = f32[4096,128]{1,0:T(8,128)} collective-permute-done((f32[4096,128]{1,0:T(8,128)}, f32[4096,128]{1,0:T(8,128)}, u32[]{:S(2)}, u32[]{:S(2)}) %collective-permute-start) | collective-permute-done | bytes 2097184 | tf_op jit(solution)/shard_map/while/body/eval_jaxpr/ppermute | solution.py:12
  496.7 22.7 %collective-permute-done = f32[4096,128]{1,0:T(8,128)} collective-permute-done((f32[4096,128]{1,0:T(8,128)}, f32[4096,128]{1,0:T(8,128)}, u32[]{:S(2)}, u32[]{:S(2)}) %collective-permute-start) | collective-permute-done | bytes 2097184 | tf_op jit(solution)/shard_map/while/body/eval_jaxpr/ppermute | solution.py:12
  542.5 22.7 %collective-permute-done = f32[4096,128]{1,0:T(8,128)} collective-permute-done((f32[4096,128]{1,0:T(8,128)}, f32[4096,128]{1,0:T(8,128)}, u32[]{:S(2)}, u32[]{:S(2)}) %collective-permute-start) | collective-permute-done | bytes 2097184 | tf_op jit(solution)/shard_map/while/body/eval_jaxpr/ppermute | solution.py:12
  588.4 24.3 %collective-permute-done = f32[4096,128]{1,0:T(8,128)} collective-permute-done((f32[4096,128]{1,0:T(8,128)}, f32[4096,128]{1,0:T(8,128)}, u32[]{:S(2)}, u32[]{:S(2)}) %collective-permute-start) | collective-permute-done | bytes 2097184 | tf_op jit(solution)/shard_map/while/body/eval_jaxpr/ppermute | solution.py:12
  634.3 26.5 %collective-permute-done = f32[4096,128]{1,0:T(8,128)} collective-permute-done((f32[4096,128]{1,0:T(8,128)}, f32[4096,128]{1,0:T(8,128)}, u32[]{:S(2)}, u32[]{:S(2)}) %collective-permute-start) | collective-permute-done | bytes 2097184 | tf_op jit(solution)/shard_map/while/body/eval_jaxpr/ppermute | solution.py:12
  680.2 28.6 %collective-permute-done = f32[4096,128]{1,0:T(8,128)} collective-permute-done((f32[4096,128]{1,0:T(8,128)}, f32[4096,128]{1,0:T(8,128)}, u32[]{:S(2)}, u32[]{:S(2)}) %collective-permute-start) | collective-permute-done | bytes 2097184 | tf_op jit(solution)/shard_map/while/body/eval_jaxpr/ppermute | solution.py:12
  728.0 28.8 %collective-permute-done = f32[4096,128]{1,0:T(8,128)} collective-permute-done((f32[4096,128]{1,0:T(8,128)}, f32[4096,128]{1,0:T(8,128)}, u32[]{:S(2)}, u32[]{:S(2)}) %collective-permute-start) | collective-permute-done | bytes 2097184 | tf_op jit(solution)/shard_map/while/body/eval_jaxpr/ppermute | solution.py:12
  781.0 8.6 fusion.10
  812.5 74.1 %reduce-scatter.2.cloned.1.call-done = f32[2048,64]{0,1:T(8,128)} async-done(((f32[2048,512]{0,1:T(8,128)}), f32[2048,64]{0,1:T(8,128)}) %reduce-scatter.2.cloned.1.call-update) | async-done | bytes 524304 | tf_op jit(solution)/shard_map/reduce_scatter | solution.py:89
  (292 shorter events, 372.8 us)
Async XLA Ops:
  7.2 797.7 %copy-start = (f32[64,512]{1,0:T(8,128)S(1)}, f32[64,512]{1,0:T(8,128)}, u32[]{:S(2)}) copy-start(f32[64,512]{1,0:T(8,128)} %param.13) | copy-start | bytes 393220
  7.2 6.6 copy-start.6
  7.2 54.1 %all-gather.2.cloned.1.call-start = ((), (), s32[]{:S(2)}) async-start(), calls=%async_computation.1 | async-start | bytes 3145728 | tf_op jit(solution)/shard_map/all_gather | solution.py:60
  7.2 6.5 copy-start.1
  13.8 5.9 copy-start.5
  13.8 6.5 copy-start.7
  19.2 867.5 %reduce-scatter.2.cloned.1.call-start = ((), (), s32[]{:S(2)}) async-start(), calls=%async_computation.2 | async-start | bytes 4718592 | tf_op jit(solution)/shard_map/reduce_scatter | solution.py:89
  71.5 6.8 copy-start.3
  80.1 26.3 %collective-permute-start = (f32[4096,128]{1,0:T(8,128)}, f32[4096,128]{1,0:T(8,128)}, u32[]{:S(2)}, u32[]{:S(2)}) collective-permute-start(f32[4096,128]{1,0:T(8,128)} %get-tuple-element.227), channel_id=1, source_target_pairs={{15,0},{0,1},{1,2},{2,3},{3,4},{4,5},{5,6},{6,7},{7,8},{8,9},{9,10... | collective-permute-start | bytes 6291464 | tf_op jit(solution)/shard_map/while/body/eval_jaxpr/ppermute | solution.py:12
  125.0 27.3 %collective-permute-start = (f32[4096,128]{1,0:T(8,128)}, f32[4096,128]{1,0:T(8,128)}, u32[]{:S(2)}, u32[]{:S(2)}) collective-permute-start(f32[4096,128]{1,0:T(8,128)} %get-tuple-element.227), channel_id=1, source_target_pairs={{15,0},{0,1},{1,2},{2,3},{3,4},{4,5},{5,6},{6,7},{7,8},{8,9},{9,10... | collective-permute-start | bytes 6291464 | tf_op jit(solution)/shard_map/while/body/eval_jaxpr/ppermute | solution.py:12
  170.9 27.3 %collective-permute-start = (f32[4096,128]{1,0:T(8,128)}, f32[4096,128]{1,0:T(8,128)}, u32[]{:S(2)}, u32[]{:S(2)}) collective-permute-start(f32[4096,128]{1,0:T(8,128)} %get-tuple-element.227), channel_id=1, source_target_pairs={{15,0},{0,1},{1,2},{2,3},{3,4},{4,5},{5,6},{6,7},{7,8},{8,9},{9,10... | collective-permute-start | bytes 6291464 | tf_op jit(solution)/shard_map/while/body/eval_jaxpr/ppermute | solution.py:12
  216.8 27.3 %collective-permute-start = (f32[4096,128]{1,0:T(8,128)}, f32[4096,128]{1,0:T(8,128)}, u32[]{:S(2)}, u32[]{:S(2)}) collective-permute-start(f32[4096,128]{1,0:T(8,128)} %get-tuple-element.227), channel_id=1, source_target_pairs={{15,0},{0,1},{1,2},{2,3},{3,4},{4,5},{5,6},{6,7},{7,8},{8,9},{9,10... | collective-permute-start | bytes 6291464 | tf_op jit(solution)/shard_map/while/body/eval_jaxpr/ppermute | solution.py:12
  262.6 27.3 %collective-permute-start = (f32[4096,128]{1,0:T(8,128)}, f32[4096,128]{1,0:T(8,128)}, u32[]{:S(2)}, u32[]{:S(2)}) collective-permute-start(f32[4096,128]{1,0:T(8,128)} %get-tuple-element.227), channel_id=1, source_target_pairs={{15,0},{0,1},{1,2},{2,3},{3,4},{4,5},{5,6},{6,7},{7,8},{8,9},{9,10... | collective-permute-start | bytes 6291464 | tf_op jit(solution)/shard_map/while/body/eval_jaxpr/ppermute | solution.py:12
  308.5 27.3 %collective-permute-start = (f32[4096,128]{1,0:T(8,128)}, f32[4096,128]{1,0:T(8,128)}, u32[]{:S(2)}, u32[]{:S(2)}) collective-permute-start(f32[4096,128]{1,0:T(8,128)} %get-tuple-element.227), channel_id=1, source_target_pairs={{15,0},{0,1},{1,2},{2,3},{3,4},{4,5},{5,6},{6,7},{7,8},{8,9},{9,10... | collective-permute-start | bytes 6291464 | tf_op jit(solution)/shard_map/while/body/eval_jaxpr/ppermute | solution.py:12
  354.4 27.3 %collective-permute-start = (f32[4096,128]{1,0:T(8,128)}, f32[4096,128]{1,0:T(8,128)}, u32[]{:S(2)}, u32[]{:S(2)}) collective-permute-start(f32[4096,128]{1,0:T(8,128)} %get-tuple-element.227), channel_id=1, source_target_pairs={{15,0},{0,1},{1,2},{2,3},{3,4},{4,5},{5,6},{6,7},{7,8},{8,9},{9,10... | collective-permute-start | bytes 6291464 | tf_op jit(solution)/shard_map/while/body/eval_jaxpr/ppermute | solution.py:12
  400.3 27.3 %collective-permute-start = (f32[4096,128]{1,0:T(8,128)}, f32[4096,128]{1,0:T(8,128)}, u32[]{:S(2)}, u32[]{:S(2)}) collective-permute-start(f32[4096,128]{1,0:T(8,128)} %get-tuple-element.227), channel_id=1, source_target_pairs={{15,0},{0,1},{1,2},{2,3},{3,4},{4,5},{5,6},{6,7},{7,8},{8,9},{9,10... | collective-permute-start | bytes 6291464 | tf_op jit(solution)/shard_map/while/body/eval_jaxpr/ppermute | solution.py:12
  446.2 27.3 %collective-permute-start = (f32[4096,128]{1,0:T(8,128)}, f32[4096,128]{1,0:T(8,128)}, u32[]{:S(2)}, u32[]{:S(2)}) collective-permute-start(f32[4096,128]{1,0:T(8,128)} %get-tuple-element.227), channel_id=1, source_target_pairs={{15,0},{0,1},{1,2},{2,3},{3,4},{4,5},{5,6},{6,7},{7,8},{8,9},{9,10... | collective-permute-start | bytes 6291464 | tf_op jit(solution)/shard_map/while/body/eval_jaxpr/ppermute | solution.py:12
  492.1 27.3 %collective-permute-start = (f32[4096,128]{1,0:T(8,128)}, f32[4096,128]{1,0:T(8,128)}, u32[]{:S(2)}, u32[]{:S(2)}) collective-permute-start(f32[4096,128]{1,0:T(8,128)} %get-tuple-element.227), channel_id=1, source_target_pairs={{15,0},{0,1},{1,2},{2,3},{3,4},{4,5},{5,6},{6,7},{7,8},{8,9},{9,10... | collective-permute-start | bytes 6291464 | tf_op jit(solution)/shard_map/while/body/eval_jaxpr/ppermute | solution.py:12
  538.0 27.3 %collective-permute-start = (f32[4096,128]{1,0:T(8,128)}, f32[4096,128]{1,0:T(8,128)}, u32[]{:S(2)}, u32[]{:S(2)}) collective-permute-start(f32[4096,128]{1,0:T(8,128)} %get-tuple-element.227), channel_id=1, source_target_pairs={{15,0},{0,1},{1,2},{2,3},{3,4},{4,5},{5,6},{6,7},{7,8},{8,9},{9,10... | collective-permute-start | bytes 6291464 | tf_op jit(solution)/shard_map/while/body/eval_jaxpr/ppermute | solution.py:12
  583.9 28.9 %collective-permute-start = (f32[4096,128]{1,0:T(8,128)}, f32[4096,128]{1,0:T(8,128)}, u32[]{:S(2)}, u32[]{:S(2)}) collective-permute-start(f32[4096,128]{1,0:T(8,128)} %get-tuple-element.227), channel_id=1, source_target_pairs={{15,0},{0,1},{1,2},{2,3},{3,4},{4,5},{5,6},{6,7},{7,8},{8,9},{9,10... | collective-permute-start | bytes 6291464 | tf_op jit(solution)/shard_map/while/body/eval_jaxpr/ppermute | solution.py:12
  631.4 29.4 %collective-permute-start = (f32[4096,128]{1,0:T(8,128)}, f32[4096,128]{1,0:T(8,128)}, u32[]{:S(2)}, u32[]{:S(2)}) collective-permute-start(f32[4096,128]{1,0:T(8,128)} %get-tuple-element.227), channel_id=1, source_target_pairs={{15,0},{0,1},{1,2},{2,3},{3,4},{4,5},{5,6},{6,7},{7,8},{8,9},{9,10... | collective-permute-start | bytes 6291464 | tf_op jit(solution)/shard_map/while/body/eval_jaxpr/ppermute | solution.py:12
  679.4 29.4 %collective-permute-start = (f32[4096,128]{1,0:T(8,128)}, f32[4096,128]{1,0:T(8,128)}, u32[]{:S(2)}, u32[]{:S(2)}) collective-permute-start(f32[4096,128]{1,0:T(8,128)} %get-tuple-element.227), channel_id=1, source_target_pairs={{15,0},{0,1},{1,2},{2,3},{3,4},{4,5},{5,6},{6,7},{7,8},{8,9},{9,10... | collective-permute-start | bytes 6291464 | tf_op jit(solution)/shard_map/while/body/eval_jaxpr/ppermute | solution.py:12
  727.4 29.4 %collective-permute-start = (f32[4096,128]{1,0:T(8,128)}, f32[4096,128]{1,0:T(8,128)}, u32[]{:S(2)}, u32[]{:S(2)}) collective-permute-start(f32[4096,128]{1,0:T(8,128)} %get-tuple-element.227), channel_id=1, source_target_pairs={{15,0},{0,1},{1,2},{2,3},{3,4},{4,5},{5,6},{6,7},{7,8},{8,9},{9,10... | collective-permute-start | bytes 6291464 | tf_op jit(solution)/shard_map/while/body/eval_jaxpr/ppermute | solution.py:12
  775.4 5.6 copy-start.4
  (1 other events, 2.7 us)
Sparse Core Ops, SparseCore 0:
  19.3 41.9 all-gather.1
  810.1 76.4 reduce-scatter.1
where the time goes:
time: 902 us; the launch traced here: 896 us
  waiting for transfers between devices  457 us (51%)
  local copies, waits for them, and re-layouts  192 us (21%)
  other arithmetic  144 us (16%)
  starting transfers between devices  50 us (6%)
  matrix products  38.4 us (4%)
  between operations  14.5 us (2%)
    ppermute x15, waiting for transfers between devices, passed_along(): return lax.ppermute(block, axis, route)  358 us
    select_n x16, other arithmetic, collect(): return jnp.where(inside[:, :, None, None], picked, tiles)  132 us
    gather x32, local copies, waits for them, and re-layouts, collect(): picked = blocks[jnp.clip(local, 0, piece_blocks - 1)]  88.1 us
    reduce_scatter x1, waiting for transfers between devices, body(): mixed = lax.psum_scatter(term, 'head', scatter_dimension=1, tiled=True)  74.1 us
    ppermute x15, starting transfers between devices, passed_along(): return lax.ppermute(block, axis, route)  49.4 us
    while x15, local copies, waits for them, and re-layouts  45.7 us
    slice x16, local copies, waits for them, and re-layouts, visit_panel(): piece = panel[replica_index * row_count:(replica_index + 1) * row_count]  27.9 us
    all_gather x1, waiting for transfers between devices, body(): panel_start = lax.all_gather(panel_own, 'replica', axis=0, tiled=True)  24.3 us
  transfers between devices with their start and end apart: 17, of which 17 were waited for; matrix products, arithmetic and copies ran while one was open for 3% of the time, Pallas kernels for 0%

commit v1 on v0

v1 whole, which is shorter than its diff:
```python
import functools

import jax
import jax.numpy as jnp
from jax import lax
from jax.experimental import pallas as pl
from jax.experimental.pallas import tpu as pltpu
from jax.sharding import PartitionSpec as P

MESH = pl.DeviceIdType.MESH
F32 = jnp.float32
BF16 = jnp.bfloat16

HEADS = 8
HD = 64
BLOCK = 256
HALF = 128
TILES = 4
OWN = 8
CHIP = 16
RING = 4
GROUP = RING * CHIP


def place():
    replica, blk = lax.axis_index("replica"), lax.axis_index("blk")
    core = lax.rem(blk, 2)
    x = lax.rem(lax.div(blk, 2), 2) * 2 + replica
    y = lax.div(blk, 4)
    return x, y, core


def device(x, y, core):
    return {"replica": lax.rem(x, 2), "blk": (y * 2 + lax.div(x, 2)) * 2 + core}


def split(value):
    high = value.astype(BF16).astype(F32)
    return high, value - high


def turned(value):
    return pltpu.roll(value, HD, 1)


def first_lanes(shape):
    return lax.broadcasted_iota(jnp.int32, shape, 1) < HD


def greet(devices):
    barrier = pltpu.get_barrier_semaphore()
    for one in devices:
        pl.semaphore_signal(barrier, inc=1, device_id=one, device_id_type=MESH)
    pl.semaphore_wait(barrier, len(devices))


def remote(src, dst, send, recv, to):
    return pltpu.make_async_remote_copy(
        src_ref=src, dst_ref=dst, send_sem=send, recv_sem=recv, device_id=to, device_id_type=MESH
    )


def project_kernel(nodes, w, grp, qcat, mine, ring_send, ring_recv, pass_send, pass_recv, sib_send, sib_recv):
    x, y, core = place()
    other = 1 - core
    sibling = device(x, y, other)

    def along(step):
        return device(lax.rem(x + step * other, RING), lax.rem(y + step * core, RING), core)

    here = x * other + y * core
    before, after = lax.rem(here + RING - 1, RING), lax.rem(here + 1, RING)
    greet([sibling, along(1), along(RING - 1)])

    w_high, w_low = split(w[...])
    w_high, w_low = w_high.astype(BF16), w_low.astype(BF16)

    @pl.loop(0, OWN)
    def _(i):
        rows = pl.ds(pl.multiple_of(i * BLOCK, BLOCK), BLOCK)
        high, low = split(nodes[rows, :])
        high, low = high.astype(BF16), low.astype(BF16)
        out = (
            jnp.dot(high, w_high, preferred_element_type=F32)
            + jnp.dot(high, w_low, preferred_element_type=F32)
            + jnp.dot(low, w_high, preferred_element_type=F32)
        )
        mine[0, i] = out[:HALF, :HALF]
        mine[1, i] = out[HALF:, :HALF]
        query = out[:, HALF:] * (1.0 / HD**0.5)
        q_high, q_low = split(query)
        qcat[rows, :HALF] = q_high.astype(BF16)
        qcat[rows, HALF:] = q_low.astype(BF16)

    def part(position, chunk):
        return grp.at[pl.ds(position * CHIP + chunk * OWN, OWN)]

    there = x * core + y * other
    to_sibling = remote(mine.at[other], part(there, core), sib_send, sib_recv, sibling)
    to_sibling.start()
    sends = []
    for way, step in enumerate((1, RING - 1)):
        send = remote(mine.at[core], part(here, core), ring_send.at[way, 0], ring_recv.at[way, 0], along(step))
        send.start()
        sends.append(send)

    @pl.loop(0, OWN)
    def _(i):
        grp[here * CHIP + core * OWN + i] = mine[core, i]

    to_sibling.wait()
    for way, step in enumerate((1, RING - 1)):
        send = remote(part(here, other), part(here, other), ring_send.at[way, 1], ring_recv.at[way, 1], along(step))
        send.start()
        sends.append(send)
    sends[0].wait_recv()
    on = remote(part(before, core), part(before, core), pass_send.at[0], pass_recv.at[0], along(1))
    on.start()
    sends[1].wait_recv()
    sends[3].wait_recv()
    back = remote(part(after, other), part(after, other), pass_send.at[1], pass_recv.at[1], along(RING - 1))
    back.start()
    sends[2].wait_recv()
    on.wait_recv()
    back.wait_recv()
    for send in sends:
        send.wait_send()
    on.wait_send()
    back.wait_send()


def attend_kernel(
    loc, grp, qcat, nodes, w_out, masks, updated, log_sums,
    big, mask_v, score, node_v, wall, attended, arrived, columns, columns_in,
    mask_sem, node_sem, ring_send, ring_recv, pass_send, pass_recv, sib_send, sib_recv,
    own_send, own_recv, wout_send, wout_recv, a_send, a_recv, b_send, b_recv,
):
    x, y, core = place()
    head = lax.axis_index("head")
    other = 1 - core
    sibling = device(x, y, other)

    def along(step):
        return device(lax.rem(x + step * core, RING), lax.rem(y + step * other, RING), core)

    here = x * core + y * other
    before, after = lax.rem(here + RING - 1, RING), lax.rem(here + 1, RING)

    def peer(step):
        return {"head": lax.rem(head + step, HEADS)}

    mask_copy = pltpu.make_async_copy(masks, mask_v, mask_sem)
    mask_copy.start()
    node_copy = pltpu.make_async_copy(nodes.at[pl.ds(pl.multiple_of(head * BLOCK, BLOCK), BLOCK)], node_v, node_sem)
    node_copy.start()
    greet([sibling, along(1), along(RING - 1)] + [peer(k) for k in range(1, HEADS)])

    def spot(position, p, chunk):
        return big.at[core, pl.ds((position * RING + p) * CHIP + chunk * OWN, OWN)]

    sends = {}
    for p in range(RING):
        for chunk in range(2):
            for way, step in enumerate((1, RING - 1)):
                part = chunk if way == 0 else 1 - chunk
                send = remote(
                    grp.at[pl.ds(p * CHIP + part * OWN, OWN)], spot(here, p, part),
                    ring_send.at[way, p, part], ring_recv.at[way, p, part], along(step),
                )
                send.start()
                sends[way, p, part] = send
    own = remote(grp, big.at[core, pl.ds(here * GROUP, GROUP)], own_send, own_recv, sibling)
    own.start()
    wouts = []
    for k in range(1, HEADS):
        send = remote(w_out, wall.at[head], wout_send.at[k - 1], wout_recv.at[k - 1], peer(k))
        send.start()
        wouts.append(send)
    wall[head] = w_out[...]

    @pl.loop(0, GROUP)
    def _(i):
        big[core, here * GROUP + i] = grp[i]

    forwards = []
    passes = []

    def forward(position, p, chunk, sem):
        send = remote(spot(position, p, chunk), spot(position, p, chunk), sib_send.at[sem], sib_recv.at[sem], sibling)
        send.start()
        forwards.append(send)

    for chunk in range(2):
        for p in range(RING):
            for way in range(2):
                part = chunk if way == 0 else 1 - chunk
                origin = before if way == 0 else after
                sends[way, p, part].wait_recv()
                if chunk == 0:
                    step = 1 if way == 0 else RING - 1
                    send = remote(
                        spot(origin, p, part), spot(origin, p, part), pass_send.at[way, p], pass_recv.at[way, p], along(step)
                    )
                    send.start()
                    passes.append((send, p, part))
                forward(origin, p, part, len(forwards))
    far = lax.rem(here + 2, RING)
    for send, p, part in passes:
        send.wait_recv()
        forward(far, p, part, len(forwards))
    mask_copy.wait()
    own.wait()
    for send in forwards:
        send.wait()
    for send in sends.values():
        send.wait_send()
    for send, _, _ in passes:
        send.wait_send()

    lanes = first_lanes((HALF, HALF))

    def a_copy(offset):
        return remote(
            attended.at[offset], arrived.at[head], a_send.at[offset], a_recv.at[offset], peer(offset)
        )

    @pl.loop(0, OWN)
    def _(s):
        odd = lax.rem(s, 2)
        offset = 4 + lax.div(s, 2) * (1 - odd) - lax.div(s + 1, 2) * odd
        row = lax.rem(head + offset, HEADS)
        rows = pl.ds(pl.multiple_of(row * BLOCK, BLOCK), BLOCK)
        query = qcat[rows, :]
        values = []
        for t in range(TILES):
            for half in range(2):
                kv = big[half, loc[half, row * TILES + t]]
                high, low = split(kv)
                keys = jnp.where(lanes, high, turned(low)).astype(BF16)
                values.append(jnp.where(lanes, turned(high), low).astype(BF16))
                found = lax.dot_general(
                    query, jnp.concatenate([keys, keys], axis=1), (((1,), (1,)), ((), ())), preferred_element_type=F32
                )
                live = mask_v[row, t, :, half * HALF : (half + 1) * HALF] != 0
                if t == 0:
                    i = lax.broadcasted_iota(jnp.int32, (BLOCK, HALF), 0)
                    j = lax.broadcasted_iota(jnp.int32, (BLOCK, HALF), 1) + half * HALF
                    live = live | (i == j)
                n = t * 2 + half
                score[:, n * HALF : (n + 1) * HALF] = jnp.where(live, found, -1e30)
        top = jnp.max(score[...], axis=1, keepdims=True)
        weights = jnp.exp(score[...] - top)
        total = jnp.sum(weights, axis=1, keepdims=True)
        high = weights.astype(BF16)
        low = (weights - high.astype(F32)).astype(BF16)
        value = jnp.concatenate(values, axis=0)
        both = jnp.dot(high, value, preferred_element_type=F32) + jnp.dot(low, value, preferred_element_type=F32)
        result = (both + turned(both)) / total
        log_sums[rows, :] = top + jnp.log(total)
        packed = jnp.where(lanes, result[:HALF], result[HALF:])

        @pl.when(offset != 0)
        def _():
            attended[offset] = packed
            a_copy(offset).start()

        @pl.when(offset == 0)
        def _():
            arrived[head] = packed

    for send in wouts:
        send.wait()
    node_copy.wait()
    for k in range(1, HEADS):
        a_copy(k).wait()
    merged = []
    for pair in range(HEADS // 2):
        one, two = arrived[2 * pair], arrived[2 * pair + 1]
        merged.append(jnp.concatenate([jnp.where(lanes, one, turned(two)), jnp.where(lanes, turned(one), two)], axis=0))
    merged = jnp.concatenate(merged, axis=1)
    m_high, m_low = split(merged)
    m_high, m_low = m_high.astype(BF16), m_low.astype(BF16)
    w_high, w_low = split(wall[...].reshape(HEADS * HD, HEADS * HD))
    w_high, w_low = w_high.astype(BF16), w_low.astype(BF16)
    mixed = node_v[...] + (
        jnp.dot(m_high, w_high, preferred_element_type=F32)
        + jnp.dot(m_high, w_low, preferred_element_type=F32)
        + jnp.dot(m_low, w_high, preferred_element_type=F32)
    )
    for pair in range(HEADS // 2):
        both = mixed[:, pair * HALF : (pair + 1) * HALF]
        up, down = both[:HALF], both[HALF:]
        columns[2 * pair] = jnp.where(lanes, up, turned(down))
        columns[2 * pair + 1] = jnp.where(lanes, turned(up), down)
    finals = []
    for k in range(1, HEADS):
        send = remote(
            columns.at[lax.rem(head + k, HEADS)], columns_in.at[head], b_send.at[k - 1], b_recv.at[k - 1], peer(k)
        )
        send.start()
        finals.append(send)
    columns_in[head] = columns[head]
    for send in finals:
        send.wait()
    for row in range(OWN):
        packed = columns_in[row]
        updated[row * BLOCK : row * BLOCK + HALF, :] = packed[:, :HD]
        updated[row * BLOCK + HALF : (row + 1) * BLOCK, :] = turned(packed)[:, :HD]


def body(nodes, w_query, w_key, w_value, w_out, tile_cols, tile_masks):
    w = jnp.concatenate([w_key, w_value, w_query, w_query], axis=1)
    vmem = pl.BlockSpec(memory_space=pltpu.VMEM)
    smem = pl.BlockSpec(memory_space=pltpu.SMEM)
    hbm = pl.BlockSpec(memory_space=pl.ANY)
    dma = pltpu.SemaphoreType.DMA
    rows = nodes.shape[0]
    grp, qcat = pl.pallas_call(
        project_kernel,
        out_shape=(
            jax.ShapeDtypeStruct((GROUP, HALF, HALF), F32),
            jax.ShapeDtypeStruct((rows, 2 * HALF), BF16),
        ),
        in_specs=[vmem, vmem],
        out_specs=(vmem, vmem),
        scratch_shapes=[
            pltpu.VMEM((2, OWN, HALF, HALF), F32),
            dma((2, 2)), dma((2, 2)), dma((2,)), dma((2,)), dma, dma,
        ],
        compiler_params=pltpu.CompilerParams(
            collective_id=0, has_side_effects=True, vmem_limit_bytes=40 * 2**20
        ),
        name="project",
    )(nodes, w)

    replica, blk, i = tile_cols // 128, (tile_cols // 8) % 16, tile_cols % 8
    x, y, core = (blk // 2) % 2 * 2 + replica, blk // 4, blk % 2
    loc = jnp.stack([(y * RING + x) * CHIP + core * OWN + i, (x * RING + y) * CHIP + core * OWN + i])
    loc = loc.reshape(2, OWN * TILES)
    updated, log_sums = pl.pallas_call(
        attend_kernel,
        out_shape=(
            jax.ShapeDtypeStruct((rows, HD), F32),
            jax.ShapeDtypeStruct((rows, 1), F32),
        ),
        in_specs=[smem, vmem, vmem, hbm, vmem, hbm],
        out_specs=(vmem, vmem),
        scratch_shapes=[
            pltpu.VMEM((2, RING * GROUP, HALF, HALF), F32),
            pltpu.VMEM((OWN, TILES, BLOCK, BLOCK), jnp.int32),
            pltpu.VMEM((BLOCK, TILES * BLOCK), F32),
            pltpu.VMEM((BLOCK, HEADS * HD), F32),
            pltpu.VMEM((HEADS, HD, HEADS * HD), F32),
            pltpu.VMEM((HEADS, HALF, HALF), F32),
            pltpu.VMEM((HEADS, HALF, HALF), F32),
            pltpu.VMEM((HEADS, HALF, HALF), F32),
            pltpu.VMEM((HEADS, HALF, HALF), F32),
            dma, dma,
            dma((2, RING, 2)), dma((2, RING, 2)), dma((2, RING)), dma((2, RING)), dma((24,)), dma((24,)),
            dma, dma, dma((HEADS - 1,)), dma((HEADS - 1,)),
            dma((HEADS,)), dma((HEADS,)), dma((HEADS - 1,)), dma((HEADS - 1,)),
        ],
        compiler_params=pltpu.CompilerParams(
            collective_id=1, has_side_effects=True, vmem_limit_bytes=60 * 2**20
        ),
        name="attend",
    )(loc, grp, qcat, nodes, w_out, tile_masks)
    return updated, log_sums


def solution(mesh):
    placed = (
        P(("replica", "blk"), None),
        P(None, "head"),
        P(None, "head"),
        P(None, "head"),
        P("head", None),
        P(("replica", "blk"), None),
        P(("replica", "blk"), None, None, None),
    )
    return jax.shard_map(
        body,
        mesh=mesh,
        in_specs=placed,
        out_specs=(P(("replica", "blk"), "head"), P(("replica", "blk"), "head")),
        check_vma=False,
    )
```

time: 902 us -> 160 us (0.18)
  waiting for transfers between devices: 457 us -> 0 us
  local copies, waits for them, and re-layouts: 192 us -> 13 us
  Pallas kernels: 0 us -> 144 us
  other arithmetic: 144 us -> 2.28 us
  starting transfers between devices: 50 us -> 0 us
  matrix products: 38.4 us -> 0 us
  between operations: 14.5 us -> 0.7 us
    ppermute x15 -> x0, waiting for transfers between devices: 358 us -> none  [passed_along(): return lax.ppermute(block, axis, route)]
    pallas_call x0 -> x2, Pallas kernels: none -> 144 us  [the longest x1 117 us: body(): pl.pallas_call(attend_kernel, out_shape=(jax.ShapeDtypeStruct((rows, HD),...]
    select_n x32 -> x0, other arithmetic: 133 us -> none  [the longest x16 132 us: collect(): return jnp.where(inside[:, :, None, None], picked, tiles)]
    gather x32 -> x0, local copies, waits for them, and re-layouts: 88.1 us -> none  [collect(): picked = blocks[jnp.clip(local, 0, piece_blocks - 1)]]
    reduce_scatter x1 -> x0, waiting for transfers between devices: 74.1 us -> none  [body(): mixed = lax.psum_scatter(term, 'head', scatter_dimension=1, tiled=True)]
    while x17 -> x0, local copies, waits for them, and re-layouts: 53.1 us -> none
    ppermute x15 -> x0, starting transfers between devices: 49.4 us -> none  [passed_along(): return lax.ppermute(block, axis, route)]
    dot_general x6 -> x0, matrix products: 38.4 us -> none  [the longest x1 8.56 us: body(): jnp.einsum('aihd,atjhd->hatij', queries, keys_now, precision=highest)]
  transfers between devices with their start and end apart: 17 -> 0, of which waited for: 17 -> 0; matrix products, arithmetic and copies ran while one was open for 3% -> 0% of each run, Pallas kernels for 0% -> 0%
where the time goes in v1:
time: 160 us
  Pallas kernels  144 us (90%)
  local copies, waits for them, and re-layouts  13 us (8%)
  other arithmetic  2.28 us (1%)
    pallas_call x1, Pallas kernels, body(): pl.pallas_call(attend_kernel, out_shape=(jax.ShapeDtypeStruct((rows, HD),...  117 us
    pallas_call x1, Pallas kernels, body(): pl.pallas_call(project_kernel, out_shape=(jax.ShapeDtypeStruct((GROUP, HA...  27 us
    unnamed x9, local copies, waits for them, and re-layouts  8.17 us
    pallas_call x2, local copies, waits for them, and re-layouts, body(): pl.pallas_call(attend_kernel, out_shape=(jax.ShapeDtypeStruct((rows, HD),...  4.49 us

profile of v1, /device:TPU:1, one launch (start us, length us, event | category | flops | bytes accessed | tf_op | source)
XLA Modules:
  0.0 160.0 jit_solution(6007105540132055514)
XLA Ops:
  0.6 0.7 add_add_fusion.1
  1.4 0.1 copy.17
  1.4 0.1 stack.9
  1.5 0.7 add_add_fusion
  2.2 0.1 copy.18
  2.3 0.1 stack.10
  2.4 0.6 pad_add_fusion.loc
  3.0 1.0 copy.21
  4.0 1.0 copy.19
  5.0 1.0 copy.20
  6.1 0.3 pad_maximum_fusion.w
  6.4 0.0 copy-start
  6.4 2.2 %copy-done = f32[2048,512]{1,0:T(8,128)S(1)} copy-done((f32[2048,512]{1,0:T(8,128)S(1)}, f32[2048,512]{1,0:T(8,128)}, u32[]{:S(2)}) %copy-start) | copy-done | bytes 4194328
  8.6 27.0 %project.1 = (f32[64,128,128]{2,1,0:T(8,128)S(1)}, bf16[2048,256]{1,0:T(8,128)(2,1)S(1)}) custom-call(f32[2048,512]{1,0:T(8,128)S(1)} %copy-done, f32[512,256]{1,0:T(8,128)S(1)} %pad_maximum_fusion.w), custom_call_target="tpu_custom_call" | custom-call | tf_op jit(solution)/shard_map/project/pallas_call | solution.py:318
  35.6 0.0 copy-start.1
  35.6 1.9 %copy-done.1 = f32[64,128,128]{2,1,0:T(8,128)} copy-done((f32[64,128,128]{2,1,0:T(8,128)}, f32[64,128,128]{2,1,0:T(8,128)S(1)}, u32[]{:S(2)}) %copy-start.1) | copy-done | bytes 4194328
  37.5 0.0 copy-start.2
  37.5 1.0 copy-done.2
  38.5 117.0 %attend.1 = (f32[2048,64]{1,0:T(8,128)}, f32[2048,1]{1,0:T(8,128)}) custom-call(s32[2,32]{1,0:T(2,128)} %pad_add_fusion.loc, f32[64,128,128]{2,1,0:T(8,128)} %copy-done.1, bf16[2048,256]{1,0:T(8,128)(2,1)} %copy-done.2, f32[2048,512]{1,0:T(8,128)} %nodes.3, f32[64,512]{1,0:T(8,128)} %w_out.1, s32[8,4,256,256]{3,2,1,0:T(8,128)} %masks.1), custom_call_target="tpu_custom_call" | custom-call | tf_op jit(solution)/shard_map/attend/pallas_call | solution.py:340
  155.6 2.3 %copy.23 = f32[2048,64]{0,1:T(8,128)} copy(f32[2048,64]{1,0:T(8,128)} %get-tuple-element.8) | data formatting | bytes 1048576 | tf_op jit(solution)/shard_map/attend/pallas_call | solution.py:340
  157.9 2.1 %copy.24 = f32[2048,1]{0,1:T(1,128)} copy(f32[2048,1]{1,0:T(8,128)} %get-tuple-element.9) | data formatting | bytes 16384 | tf_op jit(solution)/shard_map/attend/pallas_call | solution.py:340
Async XLA Ops:
  6.4 2.2 %copy-start = (f32[2048,512]{1,0:T(8,128)S(1)}, f32[2048,512]{1,0:T(8,128)}, u32[]{:S(2)}) copy-start(f32[2048,512]{1,0:T(8,128)} %nodes.3) | copy-start | bytes 12582916
  35.6 1.9 %copy-start.1 = (f32[64,128,128]{2,1,0:T(8,128)}, f32[64,128,128]{2,1,0:T(8,128)S(1)}, u32[]{:S(2)}) copy-start(f32[64,128,128]{2,1,0:T(8,128)S(1)} %get-tuple-element.4.grp) | copy-start | bytes 12582916
  37.5 1.0 copy-start.2

commit v2 on v0

v2 whole, which is shorter than its diff:
```python
import jax
import jax.numpy as jnp
from jax import lax
from jax.experimental import pallas as pl
from jax.experimental.pallas import tpu as pltpu
from jax.sharding import PartitionSpec as P

MESH = pl.DeviceIdType.MESH
F32 = jnp.float32
BF16 = jnp.bfloat16
I32 = jnp.int32

HEADS = 8
HD = 64
BLOCK = 256
HALF = 128
TILES = 4
OWN = 8
CHIP = 16
RING = 4
GROUP = RING * CHIP
BLOCKS = RING * GROUP
SLOTS = 22
PART = SLOTS // 2
NEEDS = OWN * TILES
PICK, SPOT, PLACE, MOST = 0, 8, 16, 24


def place():
    replica, blk = lax.axis_index("replica"), lax.axis_index("blk")
    core = lax.rem(blk, 2)
    x = lax.rem(lax.div(blk, 2), 2) * 2 + replica
    y = lax.div(blk, 4)
    return x, y, core


def device(x, y, core):
    return {"replica": lax.rem(x, 2), "blk": (y * 2 + lax.div(x, 2)) * 2 + core}


def first_axis(x, y, core):
    def along(step):
        return device(lax.rem(x + step * (1 - core), RING), lax.rem(y + step * core, RING), core)

    return along, x * (1 - core) + y * core


def second_axis(x, y, core):
    def along(step):
        return device(lax.rem(x + step * core, RING), lax.rem(y + step * (1 - core), RING), core)

    return along, x * core + y * (1 - core)


def peer(step):
    return {"head": lax.rem(lax.axis_index("head") + step, HEADS)}


def split(value):
    high = value.astype(BF16).astype(F32)
    return high, value - high


def turned(value):
    return pltpu.roll(value, HD, 1)


def nt(a, b):
    return lax.dot_general(a, b, (((1,), (1,)), ((), ())), preferred_element_type=F32)


def lane(shape):
    return lax.broadcasted_iota(I32, shape, 1)


def greet(devices):
    barrier = pltpu.get_barrier_semaphore()
    for one in devices:
        pl.semaphore_signal(barrier, inc=1, device_id=one, device_id_type=MESH)
    pl.semaphore_wait(barrier, len(devices))


def remote(src, dst, send, recv, to):
    return pltpu.make_async_remote_copy(
        src_ref=src, dst_ref=dst, send_sem=send, recv_sem=recv, device_id=to, device_id_type=MESH
    )


def started(*what):
    copy = remote(*what)
    copy.start()
    return copy


def project_kernel(
    nodes, wk, wv, wq, w_out, asked, grp, qcat, wall, table,
    mine, asked_in, news, news_in, most, most_in,
    ring_send, ring_recv, pass_send, pass_recv, sib_send, sib_recv, asked_send, asked_recv,
    news_send, news_recv, most_send, most_recv, wout_send, wout_recv, share_send, share_recv,
):
    x, y, core = place()
    head = lax.axis_index("head")
    other = 1 - core
    sibling = device(x, y, other)
    along, here = first_axis(x, y, core)
    across, there = second_axis(x, y, core)
    before, after = lax.rem(here + RING - 1, RING), lax.rem(here + 1, RING)
    steps = (1, 2, 3)
    greet(
        [sibling]
        + [along(k) for k in steps]
        + [across(k) for k in steps]
        + [peer(k) for k in range(1, HEADS)]
    )
    ask = started(asked, asked_in, asked_send, asked_recv, sibling)
    lines = pl.ds(pl.multiple_of(core * (HD // 2), HD // 2), HD // 2)
    wouts = [
        started(w_out.at[lines], wall.at[head, lines], wout_send.at[k], wout_recv.at[k], peer(k)) for k in range(1, HEADS)
    ]
    wall[head] = w_out[...]

    w_high, w_low = split(jnp.concatenate([wk[...], wv[...], wq[...], wq[...]], axis=0))
    w_high, w_low = w_high.astype(BF16), w_low.astype(BF16)

    @pl.loop(0, OWN)
    def _(i):
        rows = pl.ds(pl.multiple_of(i * BLOCK, BLOCK), BLOCK)
        high, low = split(nodes[rows, :])
        high, low = high.astype(BF16), low.astype(BF16)
        out = nt(high, w_high) + nt(high, w_low) + nt(low, w_high)
        mine[0, i] = out[:HALF, :HALF]
        mine[1, i] = out[HALF:, :HALF]
        q_high, q_low = split(out[:, HALF:] * (1.0 / HD**0.5))
        qcat[rows, :HALF] = q_high.astype(BF16)
        qcat[rows, HALF:] = q_low.astype(BF16)

    def part(position, chunk):
        return grp.at[pl.ds(position * CHIP + chunk * OWN, OWN)]

    to_sibling = started(mine.at[other], part(there, core), sib_send, sib_recv, sibling)
    sends = [
        started(mine.at[core], part(here, core), ring_send.at[way, 0], ring_recv.at[way, 0], along(step))
        for way, step in enumerate((1, RING - 1))
    ]

    @pl.loop(0, OWN)
    def _(i):
        grp[here * CHIP + core * OWN + i] = mine[core, i]

    to_sibling.wait()
    sends += [
        started(part(here, other), part(here, other), ring_send.at[way, 1], ring_recv.at[way, 1], along(step))
        for way, step in enumerate((1, RING - 1))
    ]

    ask.wait()
    everything = jnp.concatenate([asked[...], asked_in[...]], axis=0)

    def positions(col):
        replica, blk, i = col >> 7, (col >> 3) & 15, col & 7
        px, py, pc = ((blk >> 1) & 1) * 2 + replica, blk >> 2, blk & 1
        return (py * RING + px) * CHIP + pc * OWN + i, (px * RING + py) * CHIP + pc * OWN + i

    used = []
    for wanted in positions(everything):
        ids = lane((2 * NEEDS, HALF))
        hits = [jnp.where(wanted == ids + n * HALF, 1.0, 0.0) for n in range(BLOCKS // HALF)]
        used.append(jnp.concatenate([jnp.max(one, axis=0, keepdims=True) for one in hits], axis=1))
    line = lax.broadcasted_iota(I32, (8, BLOCKS), 0)
    used = jnp.where(line == 0, used[0], jnp.where(line == 1, used[1], 0.0))
    i, j = lax.broadcasted_iota(I32, (BLOCKS, BLOCKS), 0), lane((BLOCKS, BLOCKS))
    earlier = jnp.where((i < j) & ((i >> 6) == (j >> 6)), 1.0, 0.0).astype(BF16)
    ranks = jnp.dot(used.astype(BF16), earlier, preferred_element_type=F32)
    home = jnp.where(line == 0, y, x)
    filled = jnp.where((used > 0.5) & ((lane((8, BLOCKS)) >> 6) != home), ranks + 1.0, 0.0)
    own_most = jnp.max(jnp.max(filled, axis=0, keepdims=True), axis=1, keepdims=True)
    news[0] = used
    news[1] = ranks
    news[2] = jnp.broadcast_to(own_most, (8, BLOCKS))
    tell = [
        started(news, news_in.at[RING - k], news_send.at[k], news_recv.at[RING - k], across(k)) for k in steps
    ]

    sends[0].wait_recv()
    on = started(part(before, core), part(before, core), pass_send.at[0], pass_recv.at[0], along(1))

    column = lane((NEEDS, HALF))
    result = jnp.zeros((NEEDS, HALF), F32)
    for half, wanted in enumerate(positions(asked[...])):
        rank = jnp.zeros((NEEDS, 1), F32)
        for n in range(BLOCKS // HALF):
            row = ranks[half : half + 1, n * HALF : (n + 1) * HALF]
            rank += jnp.sum(jnp.where(wanted == column + n * HALF, row, 0.0), axis=1, keepdims=True)
        away = ((wanted >> 6) + RING - (y if half == 0 else x)) & 3
        slot = jnp.where(away == 0, (wanted & 63).astype(F32), (GROUP + (away - 1) * SLOTS).astype(F32) + rank)
        result = jnp.where(column == SPOT + half, slot, result)
        result = jnp.where(column == PLACE + half, wanted.astype(F32), result)

    for send in tell:
        send.wait()
    top = news[2]
    for k in steps:
        top = jnp.maximum(top, news_in[k, 2])
    most[...] = top
    tell_most = [
        started(most, most_in.at[RING - k], most_send.at[k], most_recv.at[RING - k], along(k)) for k in steps
    ]
    ids = lane((1, BLOCKS))
    slot = lax.broadcasted_iota(I32, (NEEDS, BLOCKS), 0).astype(F32)
    for k in steps:
        use = jnp.where(core == 0, news_in[k, 0, 0:1, :], news_in[k, 0, 1:2, :])
        rank = jnp.where(core == 0, news_in[k, 1, 0:1, :], news_in[k, 1, 1:2, :])
        rank = jnp.where((use > 0.5) & ((ids >> 6) == there), rank, -1.0)
        pick = jnp.sum(jnp.where(rank == slot, (ids & 63).astype(F32), 0.0), axis=1, keepdims=True)
        result = jnp.where(column == PICK + k, pick, result)

    sends[1].wait_recv()
    sends[3].wait_recv()
    back = started(part(after, other), part(after, other), pass_send.at[1], pass_recv.at[1], along(RING - 1))
    shares = []
    for k in range(1, HEADS):
        wouts[k - 1].wait()
        spot = wall.at[lax.rem(head + HEADS - k, HEADS), lines]
        shares.append(started(spot, spot, share_send.at[k], share_recv.at[k], sibling))
    for send in tell_most:
        send.wait()
    for k in steps:
        top = jnp.maximum(top, most_in[k])
    top = jnp.max(top[:, :HALF], axis=0, keepdims=True)
    result = jnp.where(column == MOST, top, result)
    table[...] = result.astype(I32)

    sends[2].wait_recv()
    on.wait_recv()
    back.wait_recv()
    for send in shares:
        send.wait()
    for send in sends:
        send.wait_send()
    on.wait_send()
    back.wait_send()


def prepare(nodes_v, wall, w_high, w_low, nodes_t):
    high, low = split(wall[...].reshape(HEADS * HD, HEADS * HD).T)
    w_high[...] = high.astype(BF16)
    w_low[...] = low.astype(BF16)
    nodes_t[...] = nodes_v[...].T


def finish(
    table, base, qcat, updated, log_sums, held, mask_v, w_high, w_low, nodes_t,
    score, sums, attended, arrived, columns, a_send, a_recv, b_send, b_recv,
):
    head = lax.axis_index("head")
    lanes = lane((HALF, HALF)) < HD

    def a_copy(offset):
        return remote(attended.at[offset], arrived.at[head], a_send.at[offset], a_recv.at[offset], peer(offset))

    @pl.loop(0, OWN)
    def _(s):
        odd = lax.rem(s, 2)
        offset = 4 + lax.div(s, 2) * (1 - odd) - lax.div(s + 1, 2) * odd
        row = lax.rem(head + offset, HEADS)
        rows = pl.ds(pl.multiple_of(row * BLOCK, BLOCK), BLOCK)
        query = qcat[rows, :]
        values = []
        for t in range(TILES):
            for half in range(2):
                high, low = split(held[half, table[row * TILES + t, base + half]])
                keys = jnp.where(lanes, high, turned(low)).astype(BF16)
                values.append(jnp.where(lanes, turned(high), low).astype(BF16))
                found = nt(query, jnp.concatenate([keys, keys], axis=1))
                live = mask_v[row, t, :, half * HALF : (half + 1) * HALF] != 0
                if t == 0:
                    i = lax.broadcasted_iota(I32, (BLOCK, HALF), 0)
                    live = live | (i == lane((BLOCK, HALF)) + half * HALF)
                n = t * 2 + half
                score[:, n * HALF : (n + 1) * HALF] = jnp.where(live, found, -1e30)
        top = jnp.max(score[...], axis=1, keepdims=True)
        weights = jnp.exp(score[...] - top)
        total = jnp.sum(weights, axis=1, keepdims=True)
        high = weights.astype(BF16)
        low = (weights - high.astype(F32)).astype(BF16)
        value = jnp.concatenate(values, axis=0)
        both = jnp.dot(high, value, preferred_element_type=F32) + jnp.dot(low, value, preferred_element_type=F32)
        result = (both + turned(both)) / total
        sums[...] = jnp.where(lane((BLOCK, HALF)) == row, top + jnp.log(total), sums[...])
        packed = jnp.where(lanes, result[:HALF], result[HALF:])

        @pl.when(offset != 0)
        def _():
            attended[offset] = packed
            a_copy(offset).start()

        @pl.when(offset == 0)
        def _():
            arrived[head] = packed

    for k in range(1, HEADS):
        a_copy(k).wait()
    merged = []
    for pair in range(HEADS // 2):
        one, two = arrived[2 * pair], arrived[2 * pair + 1]
        merged.append(jnp.concatenate([jnp.where(lanes, one, turned(two)), jnp.where(lanes, turned(one), two)], axis=0))
    m_high, m_low = split(jnp.concatenate(merged, axis=1))
    m_high, m_low = m_high.astype(BF16), m_low.astype(BF16)
    columns[...] = nodes_t[...] + (nt(w_high[...], m_high) + nt(w_low[...], m_high) + nt(w_high[...], m_low))
    mine = pl.ds(pl.multiple_of(head * BLOCK, BLOCK), BLOCK)
    finals = []
    for k in range(1, HEADS):
        rows = pl.ds(pl.multiple_of(lax.rem(head + k, HEADS) * HD, HD), HD)
        finals.append(started(columns.at[rows], updated.at[:, mine], b_send.at[k], b_recv.at[k], peer(k)))
    updated[:, mine] = columns[pl.ds(pl.multiple_of(head * HD, HD), HD), :]
    flat = sums[...].T
    for row in range(OWN):
        log_sums[:, row * BLOCK : (row + 1) * BLOCK] = flat[row : row + 1, :]
    for send in finals:
        send.wait()


def fetch(nodes, masks, node_v, mask_v, node_sem, mask_sem):
    start = pl.multiple_of(lax.axis_index("head") * BLOCK, BLOCK)
    node_copy = pltpu.make_async_copy(nodes.at[pl.ds(start, BLOCK)], node_v, node_sem)
    node_copy.start()
    mask_copy = pltpu.make_async_copy(masks, mask_v, mask_sem)
    mask_copy.start()
    return node_copy, mask_copy


def picked_kernel(
    table, grp, qcat, wall, nodes, masks, updated, log_sums,
    held, packets, relay, mask_v, node_v, w_high, w_low, nodes_t, score, sums, attended, arrived, columns,
    mask_sem, node_sem, own_send, own_recv, ring_send, ring_recv, far_send, far_recv, pass_send, pass_recv,
    sib_send, sib_recv, a_send, a_recv, b_send, b_recv,
):
    x, y, core = place()
    sibling = device(x, y, 1 - core)
    along, _ = second_axis(x, y, core)
    ways = (1, RING - 1)
    node_copy, mask_copy = fetch(nodes, masks, node_v, mask_v, node_sem, mask_sem)

    def fill(k):
        @pl.loop(0, SLOTS)
        def _(s):
            packets[k, s] = grp[table[s, PICK + k]]

    def spot(away, chunk):
        return held.at[core, pl.ds(GROUP + (away - 1) * SLOTS + chunk * PART, PART)]

    fill(2)
    greet([sibling, along(1), along(RING - 1)] + [peer(k) for k in range(1, HEADS)])
    fars = [
        started(packets.at[2, pl.ds(way * PART, PART)], relay.at[way], far_send.at[way], far_recv.at[way], along(step))
        for way, step in enumerate(ways)
    ]
    sends = []
    for step in ways:
        fill(step)
    for chunk in range(2):
        for way, step in enumerate(ways):
            sends.append(started(
                packets.at[step, pl.ds(chunk * PART, PART)], spot(RING - step, chunk),
                ring_send.at[way, chunk], ring_recv.at[way, chunk], along(step),
            ))
    own = started(grp, held.at[core, pl.ds(0, GROUP)], own_send, own_recv, sibling)

    @pl.loop(0, GROUP)
    def _(i):
        held[core, i] = grp[i]

    sums[...] = jnp.zeros_like(sums)
    node_copy.wait()
    prepare(node_v, wall, w_high, w_low, nodes_t)

    passes = []
    for way, step in enumerate(ways):
        fars[way].wait_recv()
        passes.append(started(relay.at[way], spot(2, way), pass_send.at[way], pass_recv.at[way], along(step)))
    forwards = []

    def forward(away, chunk):
        n = len(forwards)
        forwards.append(started(spot(away, chunk), spot(away, chunk), sib_send.at[n], sib_recv.at[n], sibling))

    for n, send in enumerate(sends):
        send.wait_recv()
        forward(RING - ways[n % 2], n // 2)
    for way in range(2):
        passes[way].wait_recv()
        forward(2, way)
    mask_copy.wait()
    own.wait()
    for send in forwards:
        send.wait()
    for send in fars + sends + passes:
        send.wait_send()
    finish(
        table, SPOT, qcat, updated, log_sums, held, mask_v, w_high, w_low, nodes_t,
        score, sums, attended, arrived, columns, a_send, a_recv, b_send, b_recv,
    )


def whole_kernel(
    table, grp, qcat, wall, nodes, masks, updated, log_sums,
    held, mask_v, node_v, w_high, w_low, nodes_t, score, sums, attended, arrived, columns,
    mask_sem, node_sem, own_send, own_recv, ring_send, ring_recv, pass_send, pass_recv,
    sib_send, sib_recv, a_send, a_recv, b_send, b_recv,
):
    x, y, core = place()
    sibling = device(x, y, 1 - core)
    along, here = second_axis(x, y, core)
    before, after, far = (lax.rem(here + k, RING) for k in (RING - 1, 1, 2))
    ways = (1, RING - 1)
    node_copy, mask_copy = fetch(nodes, masks, node_v, mask_v, node_sem, mask_sem)
    greet([sibling, along(1), along(RING - 1)] + [peer(k) for k in range(1, HEADS)])

    def spot(position, p, chunk):
        return held.at[core, pl.ds((position * RING + p) * CHIP + chunk * OWN, OWN)]

    sends = {}
    for p in range(RING):
        for chunk in range(2):
            for way, step in enumerate(ways):
                part = chunk if way == 0 else 1 - chunk
                sends[way, p, part] = started(
                    grp.at[pl.ds(p * CHIP + part * OWN, OWN)], spot(here, p, part),
                    ring_send.at[way, p, part], ring_recv.at[way, p, part], along(step),
                )
    own = started(grp, held.at[core, pl.ds(here * GROUP, GROUP)], own_send, own_recv, sibling)

    @pl.loop(0, GROUP)
    def _(i):
        held[core, here * GROUP + i] = grp[i]

    sums[...] = jnp.zeros_like(sums)
    node_copy.wait()
    prepare(node_v, wall, w_high, w_low, nodes_t)
    forwards = []
    passes = []

    def forward(position, p, chunk):
        n = len(forwards)
        one = spot(position, p, chunk)
        forwards.append(started(one, one, sib_send.at[n], sib_recv.at[n], sibling))

    for chunk in range(2):
        for p in range(RING):
            for way, step in enumerate(ways):
                part = chunk if way == 0 else 1 - chunk
                origin = before if way == 0 else after
                sends[way, p, part].wait_recv()
                if chunk == 0:
                    one = spot(origin, p, part)
                    passes.append((started(one, one, pass_send.at[way, p], pass_recv.at[way, p], along(step)), p, part))
                forward(origin, p, part)
    for send, p, part in passes:
        send.wait_recv()
        forward(far, p, part)
    mask_copy.wait()
    own.wait()
    for send in forwards:
        send.wait()
    for send in sends.values():
        send.wait_send()
    for send, _, _ in passes:
        send.wait_send()
    finish(
        table, PLACE, qcat, updated, log_sums, held, mask_v, w_high, w_low, nodes_t,
        score, sums, attended, arrived, columns, a_send, a_recv, b_send, b_recv,
    )


def body(nodes, w_query, w_key, w_value, w_out, tile_cols, tile_masks):
    vmem = pl.BlockSpec(memory_space=pltpu.VMEM)
    smem = pl.BlockSpec(memory_space=pltpu.SMEM)
    hbm = pl.BlockSpec(memory_space=pl.ANY)
    dma = pltpu.SemaphoreType.DMA
    rows = nodes.shape[0]
    scratch = pltpu.VMEM
    asked = jnp.broadcast_to(tile_cols.reshape(NEEDS, 1), (NEEDS, HALF))
    grp, qcat, wall, table = pl.pallas_call(
        project_kernel,
        out_shape=(
            jax.ShapeDtypeStruct((GROUP, HALF, HALF), F32),
            jax.ShapeDtypeStruct((rows, 2 * HALF), BF16),
            jax.ShapeDtypeStruct((HEADS, HD, HEADS * HD), F32),
            jax.ShapeDtypeStruct((NEEDS, HALF), I32),
        ),
        in_specs=[vmem] * 6,
        out_specs=(vmem,) * 4,
        scratch_shapes=[
            scratch((2, OWN, HALF, HALF), F32),
            scratch((NEEDS, HALF), I32),
            scratch((3, 8, BLOCKS), F32), scratch((RING, 3, 8, BLOCKS), F32),
            scratch((8, BLOCKS), F32), scratch((RING, 8, BLOCKS), F32),
            dma((2, 2)), dma((2, 2)), dma((2,)), dma((2,)), dma, dma, dma, dma,
            dma((RING,)), dma((RING,)), dma((RING,)), dma((RING,)),
            dma((HEADS,)), dma((HEADS,)), dma((HEADS,)), dma((HEADS,)),
        ],
        compiler_params=pltpu.CompilerParams(collective_id=0, has_side_effects=True, vmem_limit_bytes=24 * 2**20),
        name="project",
    )(nodes, w_key.T, w_value.T, w_query.T, w_out, asked)

    def second(kernel, name, number, slots, extra, semaphores, limit):
        def call(*operands):
            return pl.pallas_call(
                kernel,
                out_shape=(jax.ShapeDtypeStruct((HD, rows), F32), jax.ShapeDtypeStruct((1, rows), F32)),
                in_specs=[smem, vmem, vmem, vmem, hbm, hbm],
                out_specs=(vmem, vmem),
                scratch_shapes=[
                    scratch((2, slots, HALF, HALF), F32),
                    *extra,
                    scratch((OWN, TILES, BLOCK, BLOCK), I32),
                    scratch((BLOCK, HEADS * HD), F32),
                    scratch((HEADS * HD, HEADS * HD), BF16), scratch((HEADS * HD, HEADS * HD), BF16),
                    scratch((HEADS * HD, BLOCK), F32),
                    scratch((BLOCK, TILES * BLOCK), F32),
                    scratch((BLOCK, HALF), F32),
                    scratch((HEADS, HALF, HALF), F32), scratch((HEADS, HALF, HALF), F32),
                    scratch((HEADS * HD, BLOCK), F32),
                    dma, dma, dma, dma,
                    *semaphores,
                    dma((HEADS,)), dma((HEADS,)), dma((HEADS,)), dma((HEADS,)),
                ],
                compiler_params=pltpu.CompilerParams(
                    collective_id=number, has_side_effects=True, vmem_limit_bytes=limit * 2**20
                ),
                name=name,
            )(*operands)

        return call

    picked = second(
        picked_kernel, "picked", 1, GROUP + 3 * SLOTS,
        [scratch((RING, SLOTS, HALF, HALF), F32), scratch((2, PART, HALF, HALF), F32)],
        [dma((2, 2)), dma((2, 2)), dma((2,)), dma((2,)), dma((2,)), dma((2,)), dma((6,)), dma((6,))],
        48,
    )
    whole = second(
        whole_kernel, "whole", 2, BLOCKS, [],
        [dma((2, RING, 2)), dma((2, RING, 2)), dma((2, RING)), dma((2, RING)), dma((24,)), dma((24,))],
        60,
    )
    updated, log_sums = lax.cond(
        table[0, MOST] > SLOTS, whole, picked, table, grp, qcat, wall, nodes, tile_masks
    )
    return updated.T, log_sums.T


def solution(mesh):
    placed = (
        P(("replica", "blk"), None),
        P(None, "head"),
        P(None, "head"),
        P(None, "head"),
        P("head", None),
        P(("replica", "blk"), None),
        P(("replica", "blk"), None, None, None),
    )
    return jax.shard_map(
        body,
        mesh=mesh,
        in_specs=placed,
        out_specs=(P(("replica", "blk"), "head"), P(("replica", "blk"), "head")),
        check_vma=False,
    )
```

time: 902 us -> 121 us (0.13)
  waiting for transfers between devices: 457 us -> 0 us
  local copies, waits for them, and re-layouts: 192 us -> 6.51 us
  other arithmetic: 144 us -> 0 us
  Pallas kernels: 0 us -> 113 us
  starting transfers between devices: 50 us -> 0 us
  matrix products: 38.4 us -> 0 us
  between operations: 14.5 us -> 1.31 us
    ppermute x15 -> x0, waiting for transfers between devices: 358 us -> none  [passed_along(): return lax.ppermute(block, axis, route)]
    select_n x32 -> x0, other arithmetic: 133 us -> none  [the longest x16 132 us: collect(): return jnp.where(inside[:, :, None, None], picked, tiles)]
    pallas_call x0 -> x2, Pallas kernels: none -> 113 us  [the longest x1 74.2 us: call(): pl.pallas_call(kernel, out_shape=(jax.ShapeDtypeStruct((HD, rows), F32),...]
    gather x32 -> x0, local copies, waits for them, and re-layouts: 88.1 us -> none  [collect(): picked = blocks[jnp.clip(local, 0, piece_blocks - 1)]]
    reduce_scatter x1 -> x0, waiting for transfers between devices: 74.1 us -> none  [body(): mixed = lax.psum_scatter(term, 'head', scatter_dimension=1, tiled=True)]
    while x17 -> x0, local copies, waits for them, and re-layouts: 53.1 us -> none
    ppermute x15 -> x0, starting transfers between devices: 49.4 us -> none  [passed_along(): return lax.ppermute(block, axis, route)]
    dot_general x6 -> x0, matrix products: 38.4 us -> none  [the longest x1 8.56 us: body(): jnp.einsum('aihd,atjhd->hatij', queries, keys_now, precision=highest)]
  transfers between devices with their start and end apart: 17 -> 0, of which waited for: 17 -> 0; matrix products, arithmetic and copies ran while one was open for 3% -> 0% of each run, Pallas kernels for 0% -> 0%
where the time goes in v2:
time: 121 us; the launch traced here: 120 us
  Pallas kernels  113 us (93%)
  local copies, waits for them, and re-layouts  6.51 us (5%)
  between operations  1.31 us (1%)
    pallas_call x1, Pallas kernels, call(): pl.pallas_call(kernel, out_shape=(jax.ShapeDtypeStruct((HD, rows), F32),...  74.2 us
    pallas_call x1, Pallas kernels, body(): pl.pallas_call(project_kernel, out_shape=(jax.ShapeDtypeStruct((GROUP, HA...  38.3 us
    unnamed x11, local copies, waits for them, and re-layouts  5.77 us

profile of v2, /device:TPU:1, one launch (start us, length us, event | category | flops | bytes accessed | tf_op | source)
XLA Modules:
  0.0 120.4 jit_solution(13793395755845846573)
XLA Ops:
  0.6 0.8 copy.11
  1.4 0.1 broadcast_in_dim.7
  1.5 0.1 broadcast_in_dim.8.asked
  1.5 0.0 copy-start
  1.5 0.9 copy-done
  2.5 0.0 copy-start.1
  2.5 0.9 copy-done.1
  3.4 0.0 copy-start.2
  3.4 0.9 copy-done.2
  4.3 0.0 copy-start.3
  4.3 0.9 copy-done.3
  5.2 38.3 %project.1 = (f32[64,128,128]{2,1,0:T(8,128)}, bf16[2048,256]{1,0:T(8,128)(2,1)S(1)}, f32[8,64,512]{2,1,0:T(8,128)S(1)}, s32[32,128]{1,0:T(8,128)S(1)}) custom-call(f32[2048,512]{1,0:T(8,128)} %nodes.1, f32[64,512]{1,0:T(8,128)S(1)} %bitcast.7, f32[64,512]{1,0:T(8,128)S(1)} %bitcast.8, f32[64,512]{1,0:T(8,128)S(1)} %bitcast.9, f32[64,512]{1,0:T(8,128)S(1)} %copy-done.3, ...), custom_call_target="tpu_custom_call" | custom-call | tf_op jit(solution)/shard_map/project/pallas_call | solution.py:483
  43.5 0.6 slice.3
  44.7 74.3 %conditional.1 = (f32[64,2048]{1,0:T(8,128)S(1)}, f32[2048,1]{0,1:T(1,128)S(1)}) conditional(s32[]{:T(128)} %bitcast.5, (s32[32,128]{1,0:T(8,128)S(1)}, f32[64,128,128]{2,1,0:T(8,128)}, bf16[2048,256]{1,0:T(8,128)(2,1)S(1)}, f32[8,64,512]{2,1,0:T(8,128)S(1)}, f32[2048,512]{1,0:T(8,128)}, /*index=5*/s32[8,4,256,256]{3,2,1,0:T(8,128)}) %tuple.18, ...), branch_computations={%region_0.0_spmd, %region_1.0_spmd} | conditional | bytes 16 | solution.py:547
  44.7 74.2 %picked.1 = (f32[64,2048]{1,0:T(8,128)S(1)}, f32[1,2048]{1,0:T(1,128)S(1)}) custom-call(s32[32,128]{1,0:T(8,128)S(1)} %get-tuple-element.29.table, f32[64,128,128]{2,1,0:T(8,128)} %get-tuple-element.30.grp, bf16[2048,256]{1,0:T(8,128)(2,1)S(1)} %get-tuple-element.31.qcat, f32[8,64,512]{2,1,0:T(8,128)S(1)} %get-tuple-element.32.wall, ...), custom_call_target="tpu_custom_call" | custom-call | tf_op jit(solution)/shard_map/cond/branch_0_fun/picked/pallas_call | solution.py:508
  119.0 0.8 copy.18
  119.8 0.6 copy.19
Async XLA Ops:
  1.5 0.9 copy-start
  2.5 0.9 copy-start.1
  3.4 0.9 copy-start.2
  4.3 0.9 copy-start.3

commit v3 on v2

--- a/solution.py
+++ b/solution.py
@@ -1,3 +1,5 @@
+import functools
+
 import jax
 import jax.numpy as jnp
 from jax import lax
@@ -20,10 +22,10 @@
 RING = 4
 GROUP = RING * CHIP
 BLOCKS = RING * GROUP
-SLOTS = 22
-PART = SLOTS // 2
+SLOTS = (18, 20, 24)
+STRIDE = SLOTS[-1]
 NEEDS = OWN * TILES
-PICK, SPOT, PLACE, MOST = 0, 8, 16, 24
+PICK, SPOT, PLACE, LEVEL = 0, 8, 16, 24
 
 
 def place():
@@ -74,10 +76,12 @@
 
 
 def greet(devices):
-    barrier = pltpu.get_barrier_semaphore()
     for one in devices:
-        pl.semaphore_signal(barrier, inc=1, device_id=one, device_id_type=MESH)
-    pl.semaphore_wait(barrier, len(devices))
+        pl.semaphore_signal(pltpu.get_barrier_semaphore(), inc=1, device_id=one, device_id_type=MESH)
+
+
+def met(count):
+    pl.semaphore_wait(pltpu.get_barrier_semaphore(), count)
 
 
 def remote(src, dst, send, recv, to):
@@ -93,9 +97,9 @@
 
 
 def project_kernel(
-    nodes, wk, wv, wq, w_out, asked, grp, qcat, wall, table,
-    mine, asked_in, news, news_in, most, most_in,
-    ring_send, ring_recv, pass_send, pass_recv, sib_send, sib_recv, asked_send, asked_recv,
+    nodes, weights, asked, grp, qcat, wall, table,
+    nodes_v, w_v, mine, news, news_in, most, most_in,
+    node_sem, w_sem, ring_send, ring_recv, pass_send, pass_recv, sib_send, sib_recv,
     news_send, news_recv, most_send, most_recv, wout_send, wout_recv, share_send, share_recv,
 ):
     x, y, core = place()
@@ -104,28 +108,68 @@
     sibling = device(x, y, other)
     along, here = first_axis(x, y, core)
     across, there = second_axis(x, y, core)
+    sibling_across, _ = second_axis(x, y, other)
+    sibling_along, _ = first_axis(x, y, other)
     before, after = lax.rem(here + RING - 1, RING), lax.rem(here + 1, RING)
     steps = (1, 2, 3)
-    greet(
-        [sibling]
-        + [along(k) for k in steps]
-        + [across(k) for k in steps]
-        + [peer(k) for k in range(1, HEADS)]
-    )
-    ask = started(asked, asked_in, asked_send, asked_recv, sibling)
+    friends = [sibling] + [peer(k) for k in range(1, HEADS)]
+    for ring in (along, across, sibling_across, sibling_along):
+        friends += [ring(k) for k in steps]
+    greet(friends)
+    w_copies = [
+        pltpu.make_async_copy(weights.at[pl.ds(0, 3 * HD)], w_v.at[pl.ds(0, 3 * HD)], w_sem.at[0]),
+        pltpu.make_async_copy(weights.at[pl.ds(2 * HD, HD)], w_v.at[pl.ds(3 * HD, HD)], w_sem.at[1]),
+    ]
+    for copy in w_copies:
+        copy.start()
+
+    def node_copy(i):
+        rows = pl.ds(pl.multiple_of(i * BLOCK, BLOCK), BLOCK)
+        return pltpu.make_async_copy(nodes.at[rows], nodes_v.at[rows], node_sem.at[i])
+
+    for i in range(OWN):
+        node_copy(i).start()
+    wout_copy = pltpu.make_async_copy(weights.at[pl.ds(3 * HD, HD)], wall.at[head], w_sem.at[2])
+    wout_copy.start()
+
+    def positions(col):
+        replica, blk, i = col >> 7, (col >> 3) & 15, col & 7
+        px, py, pc = ((blk >> 1) & 1) * 2 + replica, blk >> 2, blk & 1
+        return (py * RING + px) * CHIP + pc * OWN + i, (px * RING + py) * CHIP + pc * OWN + i
+
+    column = lane((NEEDS, HALF))
+    wanted = positions(asked[...])
+    line = lax.broadcasted_iota(I32, (8, BLOCKS), 0)
+    used = jnp.zeros((8, BLOCKS), F32)
+    for half in range(2):
+        hits = [jnp.where(wanted[half] == column + n * HALF, 1.0, 0.0) for n in range(BLOCKS // HALF)]
+        row = jnp.concatenate([jnp.max(one, axis=0, keepdims=True) for one in hits], axis=1)
+        used = jnp.where(line == half, row, used)
+    news[...] = used
+    met(len(friends))
+    tells = [started(news, news_in.at[0, core], news_send.at[0, 0], news_recv.at[0, core], sibling)]
+    for k in steps:
+        for n, ring in enumerate((across, sibling_across)):
+            tells.append(started(
+                news, news_in.at[RING - k, core], news_send.at[k, n], news_recv.at[RING - k, core], ring(k)
+            ))
     lines = pl.ds(pl.multiple_of(core * (HD // 2), HD // 2), HD // 2)
+    out_lines = pl.ds(pl.multiple_of(3 * HD + core * (HD // 2), HD // 2), HD // 2)
     wouts = [
-        started(w_out.at[lines], wall.at[head, lines], wout_send.at[k], wout_recv.at[k], peer(k)) for k in range(1, HEADS)
+        started(weights.at[out_lines], wall.at[head, lines], wout_send.at[k], wout_recv.at[k], peer(k))
+        for k in range(1, HEADS)
     ]
-    wall[head] = w_out[...]
-
-    w_high, w_low = split(jnp.concatenate([wk[...], wv[...], wq[...], wq[...]], axis=0))
+
+    for copy in w_copies:
+        copy.wait()
+    w_high, w_low = split(w_v[...])
     w_high, w_low = w_high.astype(BF16), w_low.astype(BF16)
 
     @pl.loop(0, OWN)
     def _(i):
         rows = pl.ds(pl.multiple_of(i * BLOCK, BLOCK), BLOCK)
-        high, low = split(nodes[rows, :])
+        node_copy(i).wait()
+        high, low = split(nodes_v[rows, :])
         high, low = high.astype(BF16), low.astype(BF16)
         out = nt(high, w_high) + nt(high, w_low) + nt(low, w_high)
         mine[0, i] = out[:HALF, :HALF]
@@ -138,105 +182,89 @@
         return grp.at[pl.ds(position * CHIP + chunk * OWN, OWN)]
 
     to_sibling = started(mine.at[other], part(there, core), sib_send, sib_recv, sibling)
-    sends = [
-        started(mine.at[core], part(here, core), ring_send.at[way, 0], ring_recv.at[way, 0], along(step))
-        for way, step in enumerate((1, RING - 1))
-    ]
+    def send(way, chunk):
+        src = mine.at[core] if chunk == 0 else part(here, other)
+        place_there = part(here, core if chunk == 0 else other)
+        return started(src, place_there, ring_send.at[way, chunk], ring_recv.at[way, chunk], along((1, RING - 1)[way]))
+
+    sends = {(0, 0): send(0, 0)}
+    to_sibling.wait()
+    for way, chunk in ((1, 1), (0, 1), (1, 0)):
+        sends[way, chunk] = send(way, chunk)
 
     @pl.loop(0, OWN)
     def _(i):
         grp[here * CHIP + core * OWN + i] = mine[core, i]
 
-    to_sibling.wait()
-    sends += [
-        started(part(here, other), part(here, other), ring_send.at[way, 1], ring_recv.at[way, 1], along(step))
-        for way, step in enumerate((1, RING - 1))
-    ]
-
-    ask.wait()
-    everything = jnp.concatenate([asked[...], asked_in[...]], axis=0)
-
-    def positions(col):
-        replica, blk, i = col >> 7, (col >> 3) & 15, col & 7
-        px, py, pc = ((blk >> 1) & 1) * 2 + replica, blk >> 2, blk & 1
-        return (py * RING + px) * CHIP + pc * OWN + i, (px * RING + py) * CHIP + pc * OWN + i
-
-    used = []
-    for wanted in positions(everything):
-        ids = lane((2 * NEEDS, HALF))
-        hits = [jnp.where(wanted == ids + n * HALF, 1.0, 0.0) for n in range(BLOCKS // HALF)]
-        used.append(jnp.concatenate([jnp.max(one, axis=0, keepdims=True) for one in hits], axis=1))
-    line = lax.broadcasted_iota(I32, (8, BLOCKS), 0)
-    used = jnp.where(line == 0, used[0], jnp.where(line == 1, used[1], 0.0))
+    for k in range(RING):
+        for c in (core, other) if k else (other,):
+            remote(news, news_in.at[k, c], news_send.at[0, 0], news_recv.at[k, c], sibling).wait_recv()
+    for copy in tells:
+        copy.wait_send()
+    home = jnp.zeros((8, BLOCKS), I32)
+    used = jnp.zeros((8, BLOCKS), F32)
+    for k in range(RING):
+        chip = jnp.maximum(news[...], news_in[0, other]) if k == 0 else jnp.maximum(news_in[k, 0], news_in[k, 1])
+        for half, at in enumerate((lax.rem(y + k * other, RING), lax.rem(x + k * core, RING))):
+            used = jnp.where(line == 2 * k + half, chip[half : half + 1, :], used)
+            home = jnp.where(line == 2 * k + half, at, home)
     i, j = lax.broadcasted_iota(I32, (BLOCKS, BLOCKS), 0), lane((BLOCKS, BLOCKS))
     earlier = jnp.where((i < j) & ((i >> 6) == (j >> 6)), 1.0, 0.0).astype(BF16)
     ranks = jnp.dot(used.astype(BF16), earlier, preferred_element_type=F32)
-    home = jnp.where(line == 0, y, x)
     filled = jnp.where((used > 0.5) & ((lane((8, BLOCKS)) >> 6) != home), ranks + 1.0, 0.0)
-    own_most = jnp.max(jnp.max(filled, axis=0, keepdims=True), axis=1, keepdims=True)
-    news[0] = used
-    news[1] = ranks
-    news[2] = jnp.broadcast_to(own_most, (8, BLOCKS))
-    tell = [
-        started(news, news_in.at[RING - k], news_send.at[k], news_recv.at[RING - k], across(k)) for k in steps
+    top = jnp.max(jnp.max(filled, axis=0, keepdims=True), axis=1, keepdims=True)
+    most[...] = jnp.broadcast_to(top, (8, HALF))
+    tell_most = [
+        started(most, most_in.at[RING - k], most_send.at[k], most_recv.at[RING - k], along(k)) for k in steps
     ]
-
-    sends[0].wait_recv()
-    on = started(part(before, core), part(before, core), pass_send.at[0], pass_recv.at[0], along(1))
-
-    column = lane((NEEDS, HALF))
     result = jnp.zeros((NEEDS, HALF), F32)
-    for half, wanted in enumerate(positions(asked[...])):
+    for half in range(2):
         rank = jnp.zeros((NEEDS, 1), F32)
         for n in range(BLOCKS // HALF):
             row = ranks[half : half + 1, n * HALF : (n + 1) * HALF]
-            rank += jnp.sum(jnp.where(wanted == column + n * HALF, row, 0.0), axis=1, keepdims=True)
-        away = ((wanted >> 6) + RING - (y if half == 0 else x)) & 3
-        slot = jnp.where(away == 0, (wanted & 63).astype(F32), (GROUP + (away - 1) * SLOTS).astype(F32) + rank)
+            rank += jnp.sum(jnp.where(wanted[half] == column + n * HALF, row, 0.0), axis=1, keepdims=True)
+        away = ((wanted[half] >> 6) + RING - (y if half == 0 else x)) & 3
+        slot = jnp.where(away == 0, (wanted[half] & 63).astype(F32), (GROUP + (away - 1) * STRIDE).astype(F32) + rank)
         result = jnp.where(column == SPOT + half, slot, result)
-        result = jnp.where(column == PLACE + half, wanted.astype(F32), result)
-
-    for send in tell:
-        send.wait()
-    top = news[2]
-    for k in steps:
-        top = jnp.maximum(top, news_in[k, 2])
-    most[...] = top
-    tell_most = [
-        started(most, most_in.at[RING - k], most_send.at[k], most_recv.at[RING - k], along(k)) for k in steps
-    ]
+        result = jnp.where(column == PLACE + half, wanted[half].astype(F32), result)
     ids = lane((1, BLOCKS))
     slot = lax.broadcasted_iota(I32, (NEEDS, BLOCKS), 0).astype(F32)
     for k in steps:
-        use = jnp.where(core == 0, news_in[k, 0, 0:1, :], news_in[k, 0, 1:2, :])
-        rank = jnp.where(core == 0, news_in[k, 1, 0:1, :], news_in[k, 1, 1:2, :])
+        use, rank = (
+            jnp.where(core == 0, both[2 * k : 2 * k + 1, :], both[2 * k + 1 : 2 * k + 2, :]) for both in (used, ranks)
+        )
         rank = jnp.where((use > 0.5) & ((ids >> 6) == there), rank, -1.0)
         pick = jnp.sum(jnp.where(rank == slot, (ids & 63).astype(F32), 0.0), axis=1, keepdims=True)
         result = jnp.where(column == PICK + k, pick, result)
 
-    sends[1].wait_recv()
-    sends[3].wait_recv()
+    sends[0, 0].wait_recv()
+    on = started(part(before, core), part(before, core), pass_send.at[0], pass_recv.at[0], along(1))
+    sends[1, 1].wait_recv()
     back = started(part(after, other), part(after, other), pass_send.at[1], pass_recv.at[1], along(RING - 1))
     shares = []
     for k in range(1, HEADS):
         wouts[k - 1].wait()
         spot = wall.at[lax.rem(head + HEADS - k, HEADS), lines]
         shares.append(started(spot, spot, share_send.at[k], share_recv.at[k], sibling))
-    for send in tell_most:
-        send.wait()
+    for copy in tell_most:
+        copy.wait()
+    top = most[...]
     for k in steps:
         top = jnp.maximum(top, most_in[k])
-    top = jnp.max(top[:, :HALF], axis=0, keepdims=True)
-    result = jnp.where(column == MOST, top, result)
+    top = top[0:1, :]
+    level = sum(jnp.where(top > slots, 1.0, 0.0) for slots in SLOTS)
+    result = jnp.where(column == LEVEL, level, result)
     table[...] = result.astype(I32)
 
-    sends[2].wait_recv()
+    sends[0, 1].wait_recv()
+    sends[1, 0].wait_recv()
     on.wait_recv()
     back.wait_recv()
-    for send in shares:
-        send.wait()
-    for send in sends:
-        send.wait_send()
+    wout_copy.wait()
+    for copy in shares:
+        copy.wait()
+    for copy in sends.values():
+        copy.wait_send()
     on.wait_send()
     back.wait_send()
 
@@ -330,40 +358,39 @@
 
 
 def picked_kernel(
-    table, grp, qcat, wall, nodes, masks, updated, log_sums,
-    held, packets, relay, mask_v, node_v, w_high, w_low, nodes_t, score, sums, attended, arrived, columns,
-    mask_sem, node_sem, own_send, own_recv, ring_send, ring_recv, far_send, far_recv, pass_send, pass_recv,
+    slots, table, grp, qcat, wall, nodes, masks, updated, log_sums,
+    held, packets, mask_v, node_v, w_high, w_low, nodes_t, score, sums, attended, arrived, columns,
+    mask_sem, node_sem, own_send, own_recv, ring_send, ring_recv,
     sib_send, sib_recv, a_send, a_recv, b_send, b_recv,
 ):
     x, y, core = place()
     sibling = device(x, y, 1 - core)
     along, _ = second_axis(x, y, core)
-    ways = (1, RING - 1)
+    steps = (2, 1, 3)
+    friends = [sibling] + [along(k) for k in steps] + [peer(k) for k in range(1, HEADS)]
+    greet(friends)
     node_copy, mask_copy = fetch(nodes, masks, node_v, mask_v, node_sem, mask_sem)
+    part = slots // 2
 
     def fill(k):
-        @pl.loop(0, SLOTS)
+        @pl.loop(0, slots)
         def _(s):
             packets[k, s] = grp[table[s, PICK + k]]
 
     def spot(away, chunk):
-        return held.at[core, pl.ds(GROUP + (away - 1) * SLOTS + chunk * PART, PART)]
-
-    fill(2)
-    greet([sibling, along(1), along(RING - 1)] + [peer(k) for k in range(1, HEADS)])
-    fars = [
-        started(packets.at[2, pl.ds(way * PART, PART)], relay.at[way], far_send.at[way], far_recv.at[way], along(step))
-        for way, step in enumerate(ways)
+        return held.at[core, pl.ds(GROUP + (away - 1) * STRIDE + chunk * part, part)]
+
+    for step in steps:
+        fill(step)
+    met(len(friends))
+    sends = [
+        (step, chunk, started(
+            packets.at[step, pl.ds(chunk * part, part)], spot(RING - step, chunk),
+            ring_send.at[step, chunk], ring_recv.at[step, chunk], along(step),
+        ))
+        for chunk in range(2)
+        for step in steps
     ]
-    sends = []
-    for step in ways:
-        fill(step)
-    for chunk in range(2):
-        for way, step in enumerate(ways):
-            sends.append(started(
-                packets.at[step, pl.ds(chunk * PART, PART)], spot(RING - step, chunk),
-                ring_send.at[way, chunk], ring_recv.at[way, chunk], along(step),
-            ))
     own = started(grp, held.at[core, pl.ds(0, GROUP)], own_send, own_recv, sibling)
 
     @pl.loop(0, GROUP)
@@ -374,27 +401,16 @@
     node_copy.wait()
     prepare(node_v, wall, w_high, w_low, nodes_t)
 
-    passes = []
-    for way, step in enumerate(ways):
-        fars[way].wait_recv()
-        passes.append(started(relay.at[way], spot(2, way), pass_send.at[way], pass_recv.at[way], along(step)))
     forwards = []
-
-    def forward(away, chunk):
-        n = len(forwards)
-        forwards.append(started(spot(away, chunk), spot(away, chunk), sib_send.at[n], sib_recv.at[n], sibling))
-
-    for n, send in enumerate(sends):
+    for n, (step, chunk, send) in enumerate(sends):
         send.wait_recv()
-        forward(RING - ways[n % 2], n // 2)
-    for way in range(2):
-        passes[way].wait_recv()
-        forward(2, way)
+        one = spot(RING - step, chunk)
+        forwards.append(started(one, one, sib_send.at[n], sib_recv.at[n], sibling))
     mask_copy.wait()
     own.wait()
     for send in forwards:
         send.wait()
-    for send in fars + sends + passes:
+    for _, _, send in sends:
         send.wait_send()
     finish(
         table, SPOT, qcat, updated, log_sums, held, mask_v, w_high, w_low, nodes_t,
@@ -413,8 +429,10 @@
     along, here = second_axis(x, y, core)
     before, after, far = (lax.rem(here + k, RING) for k in (RING - 1, 1, 2))
     ways = (1, RING - 1)
+    friends = [sibling, along(1), along(RING - 1)] + [peer(k) for k in range(1, HEADS)]
+    greet(friends)
     node_copy, mask_copy = fetch(nodes, masks, node_v, mask_v, node_sem, mask_sem)
-    greet([sibling, along(1), along(RING - 1)] + [peer(k) for k in range(1, HEADS)])
+    met(len(friends))
 
     def spot(position, p, chunk):
         return held.at[core, pl.ds((position * RING + p) * CHIP + chunk * OWN, OWN)]
@@ -476,10 +494,12 @@
     vmem = pl.BlockSpec(memory_space=pltpu.VMEM)
     smem = pl.BlockSpec(memory_space=pltpu.SMEM)
     hbm = pl.BlockSpec(memory_space=pl.ANY)
+    far = pl.BlockSpec(memory_space=pltpu.HBM)
     dma = pltpu.SemaphoreType.DMA
     rows = nodes.shape[0]
     scratch = pltpu.VMEM
     asked = jnp.broadcast_to(tile_cols.reshape(NEEDS, 1), (NEEDS, HALF))
+    weights = jnp.concatenate([w_key.T, w_value.T, w_query.T, w_out], axis=0)
     grp, qcat, wall, table = pl.pallas_call(
         project_kernel,
         out_shape=(
@@ -488,20 +508,21 @@
             jax.ShapeDtypeStruct((HEADS, HD, HEADS * HD), F32),
             jax.ShapeDtypeStruct((NEEDS, HALF), I32),
         ),
-        in_specs=[vmem] * 6,
+        in_specs=[far, far, vmem],
         out_specs=(vmem,) * 4,
         scratch_shapes=[
+            scratch((rows, HEADS * HD), F32), scratch((4 * HD, HEADS * HD), F32),
             scratch((2, OWN, HALF, HALF), F32),
-            scratch((NEEDS, HALF), I32),
-            scratch((3, 8, BLOCKS), F32), scratch((RING, 3, 8, BLOCKS), F32),
-            scratch((8, BLOCKS), F32), scratch((RING, 8, BLOCKS), F32),
-            dma((2, 2)), dma((2, 2)), dma((2,)), dma((2,)), dma, dma, dma, dma,
-            dma((RING,)), dma((RING,)), dma((RING,)), dma((RING,)),
+            scratch((8, BLOCKS), F32), scratch((RING, 2, 8, BLOCKS), F32),
+            scratch((8, HALF), F32), scratch((RING, 8, HALF), F32),
+            dma((OWN,)), dma((3,)),
+            dma((2, 2)), dma((2, 2)), dma((2,)), dma((2,)), dma, dma,
+            dma((RING, 2)), dma((RING, 2)), dma((RING,)), dma((RING,)),
             dma((HEADS,)), dma((HEADS,)), dma((HEADS,)), dma((HEADS,)),
         ],
         compiler_params=pltpu.CompilerParams(collective_id=0, has_side_effects=True, vmem_limit_bytes=24 * 2**20),
         name="project",
-    )(nodes, w_key.T, w_value.T, w_query.T, w_out, asked)
+    )(nodes, weights, asked)
 
     def second(kernel, name, number, slots, extra, semaphores, limit):
         def call(*operands):
@@ -533,19 +554,22 @@
 
         return call
 
-    picked = second(
-        picked_kernel, "picked", 1, GROUP + 3 * SLOTS,
-        [scratch((RING, SLOTS, HALF, HALF), F32), scratch((2, PART, HALF, HALF), F32)],
-        [dma((2, 2)), dma((2, 2)), dma((2,)), dma((2,)), dma((2,)), dma((2,)), dma((6,)), dma((6,))],
+    branches = [
+        second(
+            functools.partial(picked_kernel, slots), f"picked_{slots}", 1 + n, GROUP + 3 * STRIDE,
+            [scratch((RING, slots, HALF, HALF), F32)],
+            [dma((RING, 2)), dma((RING, 2)), dma((6,)), dma((6,))],
+            40,
+        )
+        for n, slots in enumerate(SLOTS)
+    ]
+    branches.append(second(
+        whole_kernel, "whole", 1 + len(SLOTS), BLOCKS, [],
+        [dma((2, RING, 2)), dma((2, RING, 2)), dma((2, RING)), dma((2, RING)), dma((24,)), dma((24,))],
         48,
-    )
-    whole = second(
-        whole_kernel, "whole", 2, BLOCKS, [],
-        [dma((2, RING, 2)), dma((2, RING, 2)), dma((2, RING)), dma((2, RING)), dma((24,)), dma((24,))],
-        60,
-    )
-    updated, log_sums = lax.cond(
-        table[0, MOST] > SLOTS, whole, picked, table, grp, qcat, wall, nodes, tile_masks
+    ))
+    updated, log_sums = lax.switch(
+        table[0, LEVEL], branches, table, grp, qcat, wall, nodes, tile_masks
     )
     return updated.T, log_sums.T
 

time: 121 us -> 105 us (0.87)
  Pallas kernels: 113 us -> 99.6 us
  local copies, waits for them, and re-layouts: 6.51 us -> 2.89 us
  other arithmetic: 0 us -> 1.28 us
    pallas_call x1, Pallas kernels: 74.2 us -> 65.6 us  [call(): pl.pallas_call(kernel, out_shape=(jax.ShapeDtypeStruct((HD, rows), F32),...]
    pallas_call x1, Pallas kernels: 38.3 us -> 34 us  [body(): pl.pallas_call(project_kernel, out_shape=(jax.ShapeDtypeStruct((GROUP, HA...]
    unnamed x11 -> x5, local copies, waits for them, and re-layouts: 5.77 us -> 2.15 us
    concatenate x0 -> x1, other arithmetic: none -> 1.28 us  [body(): weights = jnp.concatenate([w_key.T, w_value.T, w_query.T, w_out], axis=0)]
where the time goes in v3:
time: 105 us
  Pallas kernels  99.6 us (95%)
  local copies, waits for them, and re-layouts  2.89 us (3%)
  between operations  1.31 us (1%)
  other arithmetic  1.28 us (1%)
    pallas_call x1, Pallas kernels, call(): pl.pallas_call(kernel, out_shape=(jax.ShapeDtypeStruct((HD, rows), F32),...  65.6 us
    pallas_call x1, Pallas kernels, body(): pl.pallas_call(project_kernel, out_shape=(jax.ShapeDtypeStruct((GROUP, HA...  34 us
    unnamed x5, local copies, waits for them, and re-layouts  2.15 us

profile of v3, /device:TPU:1, one launch (start us, length us, event | category | flops | bytes accessed | tf_op | source)
XLA Modules:
  0.0 105.3 jit_solution(16110119394248951141)
XLA Ops:
  0.6 0.8 copy.11
  1.4 0.1 broadcast_in_dim.7
  1.5 0.0 copy-start
  1.5 0.1 broadcast_in_dim.8.asked
  1.5 1.3 %pad_maximum_fusion.weights = f32[256,512]{1,0:T(8,128)S(1)} fusion(f32[64,512]{1,0:T(8,128)} %param.15, f32[64,512]{1,0:T(8,128)} %bitcast.10, f32[64,512]{1,0:T(8,128)} %bitcast.11, f32[64,512]{1,0:T(8,128)} %bitcast.12), kind=kLoop, calls=%fused_computation | loop fusion | flops 393216 | bytes 1048576 | tf_op jit(solution)/shard_map/concatenate | solution.py:502
  2.8 34.0 %project.1 = (f32[64,128,128]{2,1,0:T(8,128)S(1)}, bf16[2048,256]{1,0:T(8,128)(2,1)S(1)}, f32[8,64,512]{2,1,0:T(8,128)S(1)}, s32[32,128]{1,0:T(8,128)S(1)}) custom-call(f32[2048,512]{1,0:T(8,128)} %nodes.1, f32[256,512]{1,0:T(8,128)S(1)} %pad_maximum_fusion.weights, s32[32,128]{1,0:T(8,128)S(1)} %broadcast_in_dim.8.asked), custom_call_target="tpu_custom_call" | custom-call | tf_op jit(solution)/shard_map/project/pallas_call | solution.py:503
  36.9 0.6 slice.3
  38.1 0.0 copy-done
  38.1 65.8 %conditional.1 = (f32[64,2048]{1,0:T(8,128)S(1)}, f32[2048,1]{0,1:T(1,128)S(1)}) conditional(s32[]{:T(128)} %bitcast.7, (s32[32,128]{1,0:T(8,128)S(1)}, f32[64,128,128]{2,1,0:T(8,128)S(1)}, bf16[2048,256]{1,0:T(8,128)(2,1)S(1)}, f32[8,64,512]{2,1,0:T(8,128)S(1)}, f32[2048,512]{1,0:T(8,128)S(1)}, ...), branch_computations={%region_0.0_spmd, %region_1.0_spmd, %region_2.0_spmd, %region_3.0_... | conditional | bytes 16 | solution.py:571
  38.1 65.6 %picked_18.1 = (f32[64,2048]{1,0:T(8,128)S(1)}, f32[1,2048]{1,0:T(1,128)S(1)}) custom-call(s32[32,128]{1,0:T(8,128)S(1)} %get-tuple-element.57.table, f32[64,128,128]{2,1,0:T(8,128)S(1)} %get-tuple-element.58.grp, bf16[2048,256]{1,0:T(8,128)(2,1)S(1)} %get-tuple-element.59.qcat, f32[8,64,512]{2,1,0:T(8,128)S(1)} %get-tuple-element.60.wall, ...), custom_call_target="tpu_custom_call" | custom-call | tf_op jit(solution)/shard_map/cond/branch_0_fun/picked_18/pallas_call | solution.py:529
  103.9 0.8 copy.22
  104.7 0.6 copy.23
Async XLA Ops:
  1.5 36.6 %copy-start = (f32[2048,512]{1,0:T(8,128)S(1)}, f32[2048,512]{1,0:T(8,128)}, u32[]{:S(2)}) copy-start(f32[2048,512]{1,0:T(8,128)} %nodes.1) | copy-start | bytes 12582916

commit v4 on v3

--- a/solution.py
+++ b/solution.py
@@ -153,13 +153,6 @@
             tells.append(started(
                 news, news_in.at[RING - k, core], news_send.at[k, n], news_recv.at[RING - k, core], ring(k)
             ))
-    lines = pl.ds(pl.multiple_of(core * (HD // 2), HD // 2), HD // 2)
-    out_lines = pl.ds(pl.multiple_of(3 * HD + core * (HD // 2), HD // 2), HD // 2)
-    wouts = [
-        started(weights.at[out_lines], wall.at[head, lines], wout_send.at[k], wout_recv.at[k], peer(k))
-        for k in range(1, HEADS)
-    ]
-
     for copy in w_copies:
         copy.wait()
     w_high, w_low = split(w_v[...])
@@ -191,6 +184,13 @@
     to_sibling.wait()
     for way, chunk in ((1, 1), (0, 1), (1, 0)):
         sends[way, chunk] = send(way, chunk)
+
+    lines = pl.ds(pl.multiple_of(core * (HD // 2), HD // 2), HD // 2)
+    out_lines = pl.ds(pl.multiple_of(3 * HD + core * (HD // 2), HD // 2), HD // 2)
+    wouts = [
+        started(weights.at[out_lines], wall.at[head, lines], wout_send.at[k], wout_recv.at[k], peer(k))
+        for k in range(1, HEADS)
+    ]
 
     @pl.loop(0, OWN)
     def _(i):
@@ -337,7 +337,7 @@
     columns[...] = nodes_t[...] + (nt(w_high[...], m_high) + nt(w_low[...], m_high) + nt(w_high[...], m_low))
     mine = pl.ds(pl.multiple_of(head * BLOCK, BLOCK), BLOCK)
     finals = []
-    for k in range(1, HEADS):
+    for k in (4, 3, 5, 2, 6, 1, 7):
         rows = pl.ds(pl.multiple_of(lax.rem(head + k, HEADS) * HD, HD), HD)
         finals.append(started(columns.at[rows], updated.at[:, mine], b_send.at[k], b_recv.at[k], peer(k)))
     updated[:, mine] = columns[pl.ds(pl.multiple_of(head * HD, HD), HD), :]

time: 105 us -> 106 us (level)
  no operation moved by 1% of the time
where the time goes in v4:
time: 106 us
  Pallas kernels  100 us (94%)
  local copies, waits for them, and re-layouts  2.89 us (3%)
  between operations  1.31 us (1%)
  other arithmetic  1.28 us (1%)
    pallas_call x1, Pallas kernels, call(): pl.pallas_call(kernel, out_shape=(jax.ShapeDtypeStruct((HD, rows), F32),...  66.1 us
    pallas_call x1, Pallas kernels, body(): pl.pallas_call(project_kernel, out_shape=(jax.ShapeDtypeStruct((GROUP, HA...  34 us
    unnamed x5, local copies, waits for them, and re-layouts  2.15 us

profile of v4, /device:TPU:1, one launch (start us, length us, event | category | flops | bytes accessed | tf_op | source)
XLA Modules:
  0.0 105.9 jit_solution(14638623113964311415)
XLA Ops:
  0.6 0.8 copy.11
  1.4 0.1 broadcast_in_dim.7
  1.5 0.0 copy-start
  1.5 0.1 broadcast_in_dim.8.asked
  1.5 1.3 %pad_maximum_fusion.weights = f32[256,512]{1,0:T(8,128)S(1)} fusion(f32[64,512]{1,0:T(8,128)} %param.15, f32[64,512]{1,0:T(8,128)} %bitcast.10, f32[64,512]{1,0:T(8,128)} %bitcast.11, f32[64,512]{1,0:T(8,128)} %bitcast.12), kind=kLoop, calls=%fused_computation | loop fusion | flops 393216 | bytes 1048576 | tf_op jit(solution)/shard_map/concatenate | solution.py:502
  2.8 34.0 %project.1 = (f32[64,128,128]{2,1,0:T(8,128)S(1)}, bf16[2048,256]{1,0:T(8,128)(2,1)S(1)}, f32[8,64,512]{2,1,0:T(8,128)S(1)}, s32[32,128]{1,0:T(8,128)S(1)}) custom-call(f32[2048,512]{1,0:T(8,128)} %nodes.1, f32[256,512]{1,0:T(8,128)S(1)} %pad_maximum_fusion.weights, s32[32,128]{1,0:T(8,128)S(1)} %broadcast_in_dim.8.asked), custom_call_target="tpu_custom_call" | custom-call | tf_op jit(solution)/shard_map/project/pallas_call | solution.py:503
  36.9 0.6 slice.3
  38.1 0.0 copy-done
  38.1 66.4 %conditional.1 = (f32[64,2048]{1,0:T(8,128)S(1)}, f32[2048,1]{0,1:T(1,128)S(1)}) conditional(s32[]{:T(128)} %bitcast.7, (s32[32,128]{1,0:T(8,128)S(1)}, f32[64,128,128]{2,1,0:T(8,128)S(1)}, bf16[2048,256]{1,0:T(8,128)(2,1)S(1)}, f32[8,64,512]{2,1,0:T(8,128)S(1)}, f32[2048,512]{1,0:T(8,128)S(1)}, ...), branch_computations={%region_0.0_spmd, %region_1.0_spmd, %region_2.0_spmd, %region_3.0_... | conditional | bytes 16 | solution.py:571
  38.1 66.1 %picked_18.1 = (f32[64,2048]{1,0:T(8,128)S(1)}, f32[1,2048]{1,0:T(1,128)S(1)}) custom-call(s32[32,128]{1,0:T(8,128)S(1)} %get-tuple-element.57.table, f32[64,128,128]{2,1,0:T(8,128)S(1)} %get-tuple-element.58.grp, bf16[2048,256]{1,0:T(8,128)(2,1)S(1)} %get-tuple-element.59.qcat, f32[8,64,512]{2,1,0:T(8,128)S(1)} %get-tuple-element.60.wall, ...), custom_call_target="tpu_custom_call" | custom-call | tf_op jit(solution)/shard_map/cond/branch_0_fun/picked_18/pallas_call | solution.py:529
  104.5 0.8 copy.22
  105.3 0.6 copy.23
Async XLA Ops:
  1.5 36.6 %copy-start = (f32[2048,512]{1,0:T(8,128)S(1)}, f32[2048,512]{1,0:T(8,128)}, u32[]{:S(2)}) copy-start(f32[2048,512]{1,0:T(8,128)} %nodes.1) | copy-start | bytes 12582916
